TPU v7x, 32 devices: a whole 2x2x4 slice. The times are simulated.
32 devices in a mesh: rows: 8 (over z, y), chan: 4 (over x, core).
Axes of the slice: x: 2, y: 2, z: 4, core: 2. Of those that a mesh axis runs over, the one named last changes fastest.
Arguments:
- images: bfloat16 [64, 28, 28, 2016], P(('rows', 'chan')), may hold values from -6 to 6
- counts: int32 [32], replicated, may hold values from 1 to 2, as said below
- out_grad: bfloat16 [64, 14, 14, 2016], P(('rows', 'chan')), may hold values from -6 to 6
- pointwise_w: float32 [5, 2016, 2016], P(None, 'rows', 'chan'), may hold values from -0.125 to 0.125
- grouped_w: float32 [2, 9, 56, 2016], P(None, None, None, 'rows'), may hold values from -0.25 to 0.25
- squeeze_w: float32 [2, 2016, 504], P(None, 'rows'), may hold values from -0.125 to 0.125
- excite_w: float32 [2, 504, 2016], P(None, None, 'rows'), may hold values from -0.25 to 0.25
- norm_params: float32 [2, 7, 2016], P(None, None, 'rows'), may hold values from 0.25 to 1.25
- pointwise_m: float32 [5, 2016, 2016], P(None, 'rows', 'chan'), may hold values from -0.0625 to 0.0625
- grouped_m: float32 [2, 9, 56, 2016], P(None, None, None, 'rows'), may hold values from -0.125 to 0.125
- squeeze_m: float32 [2, 2016, 504], P(None, 'rows'), may hold values from -0.0625 to 0.0625
- excite_m: float32 [2, 504, 2016], P(None, None, 'rows'), may hold values from -0.125 to 0.125
- norm_m: float32 [2, 7, 2016], P(None, None, 'rows'), may hold values from -1.5 to 1.5
Outputs:
- activations: bfloat16 [64, 14, 14, 2016], P(('rows', 'chan'))
- input_grad: bfloat16 [64, 28, 28, 2016], P(('rows', 'chan'))
- layer_norms: float32 [2, 11], replicated
- grad_pointwise: float32 [5, 2016, 2016], P(None, 'rows', 'chan')
- grad_grouped: float32 [2, 9, 56, 2016], P(None, None, None, 'rows')
- grad_squeeze: float32 [2, 2016, 504], P(None, 'rows')
- grad_excite: float32 [2, 504, 2016], P(None, None, 'rows')
- grad_norm: float32 [2, 7, 2016], P(None, None, 'rows')
- moment_pointwise: float32 [5, 2016, 2016], P(None, 'rows', 'chan')
- moment_grouped: float32 [2, 9, 56, 2016], P(None, None, None, 'rows')
- moment_squeeze: float32 [2, 2016, 504], P(None, 'rows')
- moment_excite: float32 [2, 504, 2016], P(None, None, 'rows')
- moment_norm: float32 [2, 7, 2016], P(None, None, 'rows')
- new_pointwise: float32 [5, 2016, 2016], P(None, 'rows', 'chan')
- new_grouped: float32 [2, 9, 56, 2016], P(None, None, None, 'rows')
- new_squeeze: float32 [2, 2016, 504], P(None, 'rows')
- new_excite: float32 [2, 504, 2016], P(None, None, 'rows')
- new_norm: float32 [2, 7, 2016], P(None, None, 'rows')
Inputs may be any that keep to these rules, and one draw needn't show every extreme that they name: `counts`: some device holds 2 live images; live images are the first slots of a device.
All inputs are finite; a program needn't handle non-finite values.
Results may differ from a plain program's by a relative error of at most 0.025.
Values may be sent and summed in bfloat16 or wider, within the bound.
No kernel may reach another device: no remote copies, remote signals or barrier semaphores. Data moves between devices by JAX's collectives and lax.ppermute only.
A program may use at most 704 MiB of HBM per device.

v0:
```python
import jax
import jax.numpy as jnp
from jax import lax
from jax.sharding import PartitionSpec as P

GROUPS = 36
GW = 56


highest = lax.Precision.HIGHEST
epsilon = 1e-05
momentum_rate = 0.9
learn_rate = 20.0
norm_rate = 0.1
weight_decay = 5e-05
trust_coef = 0.02


def make_patches(activation, stride, side_out):
    padded = jnp.pad(activation, ((0, 0), (1, 1), (1, 1), (0, 0)))
    spanned = stride * (side_out - 1) + 1
    shifted = [
        padded[:, row_tap : row_tap + spanned : stride, col_tap : col_tap + spanned : stride, :]
        for row_tap in range(3)
        for col_tap in range(3)
    ]
    return jnp.stack(shifted, axis=3)


def grouped_forward(activation, weight, stride, side_out):
    images_here = activation.shape[0]
    channels = activation.shape[3]
    patches = make_patches(activation, stride, side_out).reshape(
        images_here, side_out, side_out, 9, GROUPS, GW
    )
    kernel = weight.reshape(9, GW, GROUPS, GW)
    result = jnp.einsum("nhwtgi,tigo->nhwgo", patches, kernel, preferred_element_type=jnp.float32)
    return (result.reshape(images_here, side_out, side_out, channels), patches)


def grouped_backward(gradient, patches, weight, stride, side_in):
    images_here = gradient.shape[0]
    side_out = gradient.shape[1]
    channels = gradient.shape[3]
    grad_groups = gradient.reshape(images_here, side_out, side_out, GROUPS, GW)
    kernel = weight.reshape(9, GW, GROUPS, GW)
    patch_grad = jnp.einsum(
        "nhwgo,tigo->nhwtgi", grad_groups, kernel, preferred_element_type=jnp.float32
    )
    kernel_grad = jnp.einsum(
        "nhwtgi,nhwgo->tigo", patches, grad_groups, preferred_element_type=jnp.float32
    )
    zeros_in = jnp.zeros((images_here, side_in, side_in, channels), jnp.float32)
    unused, unpatch = jax.vjp(lambda field: make_patches(field, stride, side_out), zeros_in)
    entry_grad = unpatch(patch_grad.reshape(images_here, side_out, side_out, 9, channels))[0]
    return (entry_grad, kernel_grad.reshape(9, GW, channels))


def norm_forward(values, keep_mask, norm_gain, norm_bias, number):
    totals = lax.psum(
        (
            jnp.sum(values * keep_mask, axis=(0, 1, 2)),
            jnp.sum(values * values * keep_mask, axis=(0, 1, 2)),
        ),
        ("rows", "chan"),
    )
    average = totals[0] / number
    spread = totals[1] / number - average * average
    inverse = lax.rsqrt(spread + epsilon)
    scaled = (values - average) * inverse
    return (keep_mask * (norm_gain * scaled + norm_bias), (scaled, inverse))


def norm_backward(upstream, keep_mask, norm_gain, stored, number):
    scaled, inverse = stored
    grad_masked = upstream * keep_mask
    gain_grad, bias_grad = lax.psum(
        (jnp.sum(grad_masked * scaled, axis=(0, 1, 2)), jnp.sum(grad_masked, axis=(0, 1, 2))),
        ("rows", "chan"),
    )
    values_grad = (
        keep_mask * norm_gain * inverse * (grad_masked - (bias_grad + scaled * gain_grad) / number)
    )
    return (values_grad, gain_grad, bias_grad)


def excite_piece(normed, squeeze, excite):
    activation = jax.nn.silu(normed)
    pooled = jnp.mean(activation, axis=(1, 2))
    squeezed = jax.nn.silu(jnp.dot(pooled, squeeze, precision=highest))
    gating = jax.nn.sigmoid(jnp.dot(squeezed, excite, precision=highest))
    return activation * gating[:, None, None, :]


def pointwise_forward(activation, column):
    extent = activation.shape
    flattened = activation.reshape(-1, extent[3])
    full_weight = lax.all_gather(column, "chan", axis=1, tiled=True)
    result = jnp.dot(flattened, full_weight, preferred_element_type=jnp.float32).astype(
        jnp.bfloat16
    )
    stored = (flattened, full_weight)
    return (result.reshape(extent[:3] + (result.shape[1],)), stored)


def pointwise_backward(gradient, stored):
    extent = gradient.shape
    flat_grad = gradient.reshape(-1, extent[3])
    contract_rows = (((0,), (0,)), ((), ()))
    contract_cols = (((1,), (1,)), ((), ()))
    flattened, full_weight = stored
    input_flat = lax.dot_general(
        flat_grad, full_weight, contract_cols, preferred_element_type=jnp.float32
    )
    whole_grad = lax.dot_general(
        flattened, flat_grad, contract_rows, preferred_element_type=jnp.float32
    )
    column_grad = lax.psum_scatter(whole_grad, "chan", scatter_dimension=1, tiled=True)
    return (input_flat.reshape(extent[:3] + (input_flat.shape[1],)), column_grad)


def lars_step(weight, moment, gradient, ratios):
    scaled_rate = ratios.reshape((-1,) + (1,) * (weight.ndim - 1))
    moment_new = momentum_rate * moment + learn_rate * scaled_rate * (
        gradient + weight_decay * weight
    )
    return (moment_new, weight - moment_new)


def squares(tensor, weighting):
    return weighting * jnp.sum(tensor * tensor, axis=tuple(range(1, tensor.ndim)))


def per_device(
    images,
    counts,
    out_grad,
    pointwise_w,
    grouped_w,
    squeeze_w,
    excite_w,
    norm_params,
    pointwise_m,
    grouped_m,
    squeeze_m,
    excite_m,
    norm_m,
):
    slot_count = images.shape[0]
    side_in = images.shape[1]
    side_out = out_grad.shape[1]
    device_index = lax.axis_index("rows") * lax.axis_size("chan") + lax.axis_index("chan")
    own_count = lax.dynamic_index_in_dim(counts, device_index, keepdims=False)
    keep_mask = (jnp.arange(slot_count, dtype=jnp.int32) < own_count).astype(jnp.float32)[
        :, None, None, None
    ]
    live_total = jnp.sum(counts).astype(jnp.float32)
    inner_count = live_total * side_in * side_in
    outer_count = live_total * side_out * side_out
    pointwise_full, grouped_full = (
        lax.all_gather(pointwise_w.astype(jnp.bfloat16), "rows", axis=1, tiled=True),
        lax.all_gather(grouped_w.astype(jnp.bfloat16), "rows", axis=3, tiled=True),
    )
    squeeze_full, excite_full, norm_full = (
        lax.all_gather(squeeze_w, "rows", axis=1, tiled=True),
        lax.all_gather(excite_w, "rows", axis=2, tiled=True),
        lax.all_gather(norm_params, "rows", axis=2, tiled=True),
    )
    source = images * keep_mask.astype(jnp.bfloat16)

    def branch_forward(entry, conv_first, conv_last, layer, norm_first, stride, entry_count):
        expanded, keep_first = pointwise_forward(entry, pointwise_full[conv_first])
        normed_a, stored_a = norm_forward(
            expanded.astype(jnp.float32),
            keep_mask,
            norm_full[0, norm_first],
            norm_full[1, norm_first],
            entry_count,
        )
        hidden, silu_back = jax.vjp(jax.nn.silu, normed_a)
        mixed, patches = grouped_forward(
            hidden.astype(jnp.bfloat16), grouped_full[layer], stride, side_out
        )
        normed_b, stored_b = norm_forward(
            mixed,
            keep_mask,
            norm_full[0, norm_first + 1],
            norm_full[1, norm_first + 1],
            outer_count,
        )
        excited, excite_back = jax.vjp(
            excite_piece, normed_b, squeeze_full[layer], excite_full[layer]
        )
        narrowed, keep_last = pointwise_forward(
            excited.astype(jnp.bfloat16), pointwise_full[conv_last]
        )
        normed_c, stored_c = norm_forward(
            narrowed.astype(jnp.float32),
            keep_mask,
            norm_full[0, norm_first + 2],
            norm_full[1, norm_first + 2],
            outer_count,
        )
        return (
            normed_c,
            (keep_first, stored_a, silu_back, patches, stored_b, excite_back, keep_last, stored_c),
        )

    def branch_backward(grad_out, memory_kept, norm_first, layer, stride, entry_side, entry_count):
        keep_first, stored_a, silu_back, patches, stored_b, excite_back, keep_last, stored_c = (
            memory_kept
        )
        grad_c, gain_c, bias_c = norm_backward(
            grad_out, keep_mask, norm_full[0, norm_first + 2], stored_c, outer_count
        )
        grad_excited, last_column = pointwise_backward(grad_c.astype(jnp.bfloat16), keep_last)
        grad_normed_b, grad_squeeze, grad_excite = excite_back(grad_excited)
        grad_b, gain_b, bias_b = norm_backward(
            grad_normed_b, keep_mask, norm_full[0, norm_first + 1], stored_b, outer_count
        )
        grad_hidden, grad_kernel = grouped_backward(
            grad_b.astype(jnp.bfloat16), patches, grouped_full[layer], stride, entry_side
        )
        grad_normed_a = silu_back(grad_hidden)[0]
        grad_a, gain_a, bias_a = norm_backward(
            grad_normed_a, keep_mask, norm_full[0, norm_first], stored_a, entry_count
        )
        grad_entry, first_column = pointwise_backward(grad_a.astype(jnp.bfloat16), keep_first)
        return (
            grad_entry,
            first_column,
            last_column,
            grad_kernel,
            grad_squeeze,
            grad_excite,
            (gain_a, gain_b, gain_c),
            (bias_a, bias_b, bias_c),
        )

    main_one, memory_one = branch_forward(source, 0, 1, 0, 0, 2, inner_count)
    projected, keep_proj = pointwise_forward(source[:, ::2, ::2, :], pointwise_full[2])
    normed_proj, stored_proj = norm_forward(
        projected.astype(jnp.float32), keep_mask, norm_full[0, 3], norm_full[1, 3], outer_count
    )
    middle, join_one = jax.vjp(
        lambda left_in, right_in: jax.nn.silu(left_in + right_in), main_one, normed_proj
    )
    main_two, memory_two = branch_forward(middle.astype(jnp.bfloat16), 3, 4, 1, 4, 1, outer_count)
    final, join_two = jax.vjp(
        lambda left_in, right_in: jax.nn.silu(left_in + right_in), main_two, middle
    )
    activations = final.astype(jnp.bfloat16)
    grad_main_two, grad_middle = join_two(out_grad.astype(jnp.float32))
    back_two = branch_backward(grad_main_two, memory_two, 4, 1, 1, side_out, outer_count)
    grad_middle = grad_middle + back_two[0]
    grad_main_one, grad_proj_in = join_one(grad_middle)
    grad_proj, gain_proj, bias_proj = norm_backward(
        grad_proj_in, keep_mask, norm_full[0, 3], stored_proj, outer_count
    )
    grad_strided, proj_column = pointwise_backward(grad_proj.astype(jnp.bfloat16), keep_proj)
    back_one = branch_backward(grad_main_one, memory_one, 0, 0, 2, side_in, inner_count)
    grad_source = back_one[0].at[:, ::2, ::2, :].add(grad_strided)
    input_grad = (grad_source * keep_mask).astype(jnp.bfloat16)
    grad_columns = jnp.stack([back_one[1], back_one[2], proj_column, back_two[1], back_two[2]])
    grad_kernels = jnp.stack([back_one[3], back_two[3]])
    grad_squeezes = jnp.stack([back_one[4], back_two[4]])
    grad_excites = jnp.stack([back_one[5], back_two[5]])
    gains_all = jnp.stack(list(back_one[6]) + [gain_proj] + list(back_two[6]))
    biases_all = jnp.stack(list(back_one[7]) + [bias_proj] + list(back_two[7]))
    norm_grad_full = jnp.stack([gains_all, biases_all])
    rows_width = norm_params.shape[2]
    grad_norm = lax.dynamic_slice_in_dim(
        norm_grad_full, lax.axis_index("rows") * rows_width, rows_width, 2
    )
    grad_pointwise, kernel_part, squeeze_part, excite_part = (
        lax.psum_scatter(grad_columns, "rows", scatter_dimension=1, tiled=True),
        lax.psum_scatter(grad_kernels, "rows", scatter_dimension=3, tiled=True),
        lax.psum_scatter(grad_squeezes, "rows", scatter_dimension=1, tiled=True),
        lax.psum_scatter(grad_excites, "rows", scatter_dimension=2, tiled=True),
    )
    grad_grouped, grad_squeeze, grad_excite = lax.psum(
        (kernel_part, squeeze_part, excite_part), "chan"
    )
    leader = (lax.axis_index("chan") == 0).astype(jnp.float32)
    weight_terms = jnp.concatenate(
        [
            squares(pointwise_w, 1.0),
            squares(grouped_w, leader),
            squares(squeeze_w, leader),
            squares(excite_w, leader),
        ]
    )
    grad_terms = jnp.concatenate(
        [
            squares(grad_pointwise, 1.0),
            squares(grad_grouped, leader),
            squares(grad_squeeze, leader),
            squares(grad_excite, leader),
        ]
    )
    weight_sums, grad_sums = lax.psum((weight_terms, grad_terms), ("rows", "chan"))
    weight_norms = jnp.sqrt(weight_sums)
    grad_norms = jnp.sqrt(grad_sums)
    trust_ratio = trust_coef * weight_norms / (grad_norms + weight_decay * weight_norms)
    moment_pointwise, new_pointwise = lars_step(
        pointwise_w, pointwise_m, grad_pointwise, trust_ratio[0:5]
    )
    moment_grouped, new_grouped = lars_step(grouped_w, grouped_m, grad_grouped, trust_ratio[5:7])
    moment_squeeze, new_squeeze = lars_step(squeeze_w, squeeze_m, grad_squeeze, trust_ratio[7:9])
    moment_excite, new_excite = lars_step(excite_w, excite_m, grad_excite, trust_ratio[9:11])
    moment_norm = momentum_rate * norm_m + norm_rate * grad_norm
    new_norm = norm_params - moment_norm
    layer_norms = jnp.stack([weight_norms, grad_norms])
    return (
        activations,
        input_grad,
        layer_norms,
        grad_pointwise,
        grad_grouped,
        grad_squeeze,
        grad_excite,
        grad_norm,
        moment_pointwise,
        moment_grouped,
        moment_squeeze,
        moment_excite,
        moment_norm,
        new_pointwise,
        new_grouped,
        new_squeeze,
        new_excite,
        new_norm,
    )


def solution(mesh):
    in_specs = (
        P(("rows", "chan"), None, None, None),
        P(),
        P(("rows", "chan"), None, None, None),
        P(None, "rows", "chan"),
        P(None, None, None, "rows"),
        P(None, "rows", None),
        P(None, None, "rows"),
        P(None, None, "rows"),
        P(None, "rows", "chan"),
        P(None, None, None, "rows"),
        P(None, "rows", None),
        P(None, None, "rows"),
        P(None, None, "rows"),
    )
    out_specs = (
        P(("rows", "chan"), None, None, None),
        P(("rows", "chan"), None, None, None),
        P(),
        P(None, "rows", "chan"),
        P(None, None, None, "rows"),
        P(None, "rows", None),
        P(None, None, "rows"),
        P(None, None, "rows"),
        P(None, "rows", "chan"),
        P(None, None, None, "rows"),
        P(None, "rows", None),
        P(None, None, "rows"),
        P(None, None, "rows"),
        P(None, "rows", "chan"),
        P(None, None, None, "rows"),
        P(None, "rows", None),
        P(None, None, "rows"),
        P(None, None, "rows"),
    )
    return jax.shard_map(
        per_device, mesh=mesh, in_specs=in_specs, out_specs=out_specs, check_vma=False
    )
```

profile of v0, /device:TPU:0, one launch (start us, length us, event | category | flops | bytes accessed | tf_op | source)
XLA Modules:
  0.0 5094.4 jit_solution(15387719176555853558)
XLA Ops:
  18.9 221.8 %all-gather.15.cloned.1.call-done = bf16[5,2016,504]{2,0,1:T(8,128)(2,1)} async-done(((bf16[5,252,504]{2,0,1:T(8,128)(2,1)}), bf16[5,2016,504]{2,0,1:T(8,128)(2,1)}) %all-gather.15.cloned.1.call-update) | async-done | bytes 10160656 | tf_op jit(solution)/shard_map/all_gather | solution.py:161
  240.7 45.2 fusion.232
  286.0 16.0 copy.368
  362.6 16.5 slice.177
  391.9 54.3 %all_gather.30 = f32[2,7,2016]{1,0,2:T(2,128)S(1)} all-gather(f32[2,7,252]{1,0,2:T(2,128)S(1)} %copy.365), channel_id=1, replica_groups=mesh['rows'=8,'chan'=4] {'rows'}, dimensions={2}, use_global_device_ids=true | all-gather | bytes 127008 | tf_op jit(solution)/shard_map/all_gather | solution.py:167
  446.2 103.6 %slice_reduce_fusion.13 = (f32[2016]{0:T(1024)}, f32[2016]{0:T(1024)}, f32[2016]{0:T(1024)S(1)}, f32[2016]{0:T(1024)S(1)}, f32[2016]{0:T(1024)}, /*index=5*/f32[...) fusion(f32[2,7,2016]{1,0,2:T(2,128)S(1)} %all_gather.30), kind=kLoop, calls=%fused_computation.297 | loop fusion | bytes 225792 | tf_op jit(solution)/shard_map/slice | solution.py:200
  557.5 19.0 fusion.233
  576.6 19.8 copy.410
  596.5 19.9 copy.381
  630.0 24.2 fusion.234
  666.9 16.0 copy.415
  682.9 65.7 %all-gather.23.cloned.1.call-done = bf16[1,2016,2016]{1,0,2:T(2,128)(2,1)} async-done(((bf16[1,2016,504]{1,0,2:T(2,128)(2,1)}), bf16[1,2016,2016]{1,0,2:T(2,128)(2,1)}) %all-gather.23.cloned.1.call-update) | async-done | bytes 8128528 | tf_op jit(solution)/shard_map/all_gather | solution.py:98
  748.6 39.6 copy.369
  788.2 20.7 multiply_reduce_fusion.2
  822.2 39.7 all-reduce.36
  862.0 23.1 multiply_convert_fusion.2
  885.2 18.4 fusion.236
  1005.5 21.1 multiply_reduce_fusion.8
  1026.8 41.5 all-reduce.35
  1106.4 39.0 copy.390
  1154.4 39.5 copy.388
  1205.7 40.7 all-reduce.34
  1246.5 39.0 copy.392
  1311.1 40.4 all-reduce.33
  1448.5 21.3 multiply_reduce_fusion.5
  1493.9 40.2 all-reduce.32
  1555.6 39.3 copy.416
  1609.1 40.3 all-reduce.31
  1660.3 40.0 all-reduce.30
  1744.6 41.1 all-reduce.29
  1797.0 31.8 convolution_bitcast_fusion.1
  1828.9 56.9 %copy.544 = f32[2,14,14,9,36,56]{5,4,2,1,0,3:T(8,128)} copy(f32[2,14,14,9,36,56]{5,2,3,1,0,4:T(8,128)} %convolution_bitcast_fusion.1) | data formatting | bytes 56899584 | tf_op jit(solution)/shard_map/reshape | solution.py:55
  1885.8 57.7 %reshape.653 = f32[2,14,14,9,2016]{4,2,1,0,3:T(8,128)} reshape(f32[2,14,14,9,36,56]{5,4,2,1,0,3:T(8,128)} %copy.544) | data formatting | bytes 56899584 | tf_op jit(solution)/shard_map/reshape | solution.py:55
  1943.4 21.1 slice_bitcast_fusion.8
  1980.8 40.3 all-reduce.28
  2040.2 40.4 all-reduce.27
  2116.1 40.5 all-reduce.26
  2168.7 32.3 convolution_bitcast_fusion
  2201.0 56.9 %copy.547 = f32[2,14,14,9,36,56]{5,4,0,2,1,3:T(8,128)} copy(f32[2,14,14,9,36,56]{5,2,3,1,0,4:T(8,128)} %convolution_bitcast_fusion) | data formatting | bytes 56899584 | tf_op jit(solution)/shard_map/reshape | solution.py:55
  2257.9 68.6 %reshape.654 = f32[2,14,14,9,2016]{4,0,2,1,3:T(2,128)} reshape(f32[2,14,14,9,36,56]{5,4,0,2,1,3:T(8,128)} %copy.547) | data formatting | bytes 56899584 | tf_op jit(solution)/shard_map/reshape | solution.py:55
  2336.7 28.2 slice_bitcast_fusion.16
  2364.9 93.4 %pad.85 = f32[2,30,30,2016]{3,0,2,1:T(2,128)} pad(f32[2,14,14,2016]{3,0,2,1:T(2,128)} %get-tuple-element.216, f32[]{:T(128)} %constant.28.clone.1), padding=0_0_0x2_1_1x1_2_1x0_0_0 | pad | bytes 17676292 | tf_op jit(solution)/shard_map/transpose(jvp())/pad | solution.py:23
  2458.4 92.8 %pad.121 = f32[2,28,28,2016]{3,0,2,1:T(2,128)} pad(f32[2,14,14,2016]{3,0,2,1:T(2,128)} %get-tuple-element.221, f32[]{:T(128)} %constant.28.clone.1), padding=0_0_0x0_1_1x0_1_1x0_0_0 | pad | bytes 15805444 | tf_op jit(solution)/shard_map/transpose(jvp(jit(_pad)))/pad | solution.py:20
  2551.2 92.7 %pad.120 = f32[2,28,28,2016]{3,0,2,1:T(2,128)} pad(f32[2,14,14,2016]{3,0,2,1:T(2,128)} %get-tuple-element.222, f32[]{:T(128)} %constant.28.clone.1), padding=0_0_0x0_1_1x1_0_1x0_0_0 | pad | bytes 15805444 | tf_op jit(solution)/shard_map/transpose(jvp(jit(_pad)))/pad | solution.py:20
  2643.8 92.8 %pad.204 = f32[2,29,28,2016]{3,0,2,1:T(2,128)} pad(f32[2,14,14,2016]{3,0,2,1:T(2,128)} %get-tuple-element.218, f32[]{:T(128)} %constant.28.clone.1), padding=0_0_0x0_2_1x0_1_1x0_0_0 | pad | bytes 16257028
  2736.7 92.9 %pad.205 = f32[2,29,28,2016]{3,0,2,1:T(2,128)} pad(f32[2,14,14,2016]{3,0,2,1:T(2,128)} %get-tuple-element.219, f32[]{:T(128)} %constant.28.clone.1), padding=0_0_0x0_2_1x1_0_1x0_0_0 | pad | bytes 16257028
  2829.5 92.9 %pad.206 = f32[2,28,29,2016]{3,0,2,1:T(2,128)} pad(f32[2,14,14,2016]{3,0,2,1:T(2,128)} %get-tuple-element.220, f32[]{:T(128)} %constant.28.clone.1), padding=0_0_0x0_1_1x0_2_1x0_0_0 | pad | bytes 16257028
  2922.4 65.5 %pad.203 = f32[2,29,29,2016]{3,0,2,1:T(2,128)} pad(f32[2,14,14,2016]{3,0,2,1:T(2,128)S(1)} %get-tuple-element.217, f32[]{:T(128)} %constant.28.clone.1), padding=0_0_0x0_2_1x0_2_1x0_0_0 | pad | bytes 16724740
  2988.0 93.8 %pad.86 = f32[2,30,30,2016]{3,0,2,1:T(2,128)} pad(f32[2,14,14,2016]{3,0,2,1:T(2,128)} %get-tuple-element.223, f32[]{:T(128)} %constant.28.clone.1), padding=0_0_0x2_1_1x0_3_1x0_0_0 | pad | bytes 17676292 | tf_op jit(solution)/shard_map/transpose(jvp())/pad | solution.py:23
  3081.7 65.8 %pad.84 = f32[2,30,30,2016]{3,0,2,1:T(2,128)} pad(f32[2,14,14,2016]{3,0,2,1:T(2,128)S(1)} %copy-done.35, f32[]{:T(128)} %constant.28.clone.1), padding=0_0_0x2_1_1x2_1_1x0_0_0 | pad | bytes 17676292 | tf_op jit(solution)/shard_map/transpose(jvp())/pad | solution.py:23
  3147.5 22.0 add_add_fusion
  3169.6 53.6 %fusion.217 = (f32[2016]{0:T(1024)S(1)}, f32[2016]{0:T(1024)S(1)}, f32[2,28,28,2016]{3,0,2,1:T(2,128)}) fusion(f32[2016]{0:T(1024)S(1)} %copy-done.67, f32[2016]{0:T(1024)S(1)} %copy-done.83, f32[2,28,28,2016]{3,2,1,0:T(8,128)} %reshape.584, f32[2016]{0:T(1024)S(1)} %copy-done.108, f32[2016]{0:T(1024)S(1)} %copy-done.78, f32[2]{0:T(128)S(1)} %copy-done.99, ...), kind=kLoop, calls=%fused_computation.382 | loop fusion | flops 75862080 | bytes 113847560 | tf_op jit(solution)/shard_map/reduce_sum | solution.py:78
  3223.2 41.3 all-reduce.25
  3264.5 22.2 multiply_convert_fusion.1
  3289.5 30.5 convolution_bitcast_fusion.2
  3338.3 22.7 fusion.94
  3382.0 20.4 fusion.89
  3432.0 16.9 copy.458
  3489.9 81.2 %reduce-scatter.23.cloned.1.call-done = f32[504,2016]{1,0:T(8,128)} async-done(((f32[2016,2016]{1,0:T(8,128)}), f32[504,2016]{1,0:T(8,128)}) %reduce-scatter.23.cloned.1.call-update) | async-done | bytes 4064272
  3622.6 24.6 fusion.15
  3658.4 32.2 scatter_fusion
  3690.6 1251.7 %all-reduce.42.cloned.1.call-done = (f32[2,504,2016]{2,1,0:T(8,128)}, f32[2,2016,504]{2,0,1:T(2,128)}, f32[2,9,56,2016]{3,2,1,0:T(8,128)}, f32[5,2016,504]{2,1,0:T(8,128)}) async-done(((f32[2,504,2016]{2,1,0:T(8,128)}, f32[2,2016,504]{2,0,1:T(2,128)}, f32[2,9,56,2016]{3,2,1,0:T(8,128)}, f32[5,2016,504]{2,1,0:T(8,128)}), (f32[2,504,2016]{2,1,0:T(8,128)}, f32[2,2016,504]{2,0,1:T(2,128)}, ...) | async-done | bytes 44706832
  4960.6 57.1 %all-reduce.44.cloned.1.call-done = (f32[2,504,252]{2,1,0:T(8,128)}, f32[2,252,504]{2,0,1:T(2,128)}, f32[2,9,56,252]{3,2,1,0:T(8,128)}) async-done(((f32[2,504,252]{2,1,0:T(8,128)}, f32[2,252,504]{2,0,1:T(2,128)}, f32[2,9,56,252]{3,2,1,0:T(8,128)}), (f32[2,504,252]{2,1,0:T(8,128)}, f32[2,252,504]{2,0,1:T(2,128)}, f32[2,9,56,252]{3,2,1,0:T(8,128)})) %all-reduce.44.cloned.1.call-update) | async-done | bytes 3048208 | tf_op jit(solution)/shard_map/psum | solution.py:281
  5025.2 39.5 all-reduce.24
  (612 shorter events, 856.5 us)
Async XLA Ops:
  7.2 233.5 %all-gather.15.cloned.1.call-start = ((), (), s32[]{:S(2)}) async-start(), calls=%async_computation.5 | async-start | bytes 18579456 | tf_op jit(solution)/shard_map/all_gather | solution.py:161
  13.5 544.0 %all-gather.17.cloned.1.call-start = ((), (), s32[]{:S(2)}) async-start(), calls=%async_computation.6 | async-start | bytes 10450944 | tf_op jit(solution)/shard_map/all_gather | solution.py:162
  16.6 613.4 %all-gather.19.cloned.1.call-start = ((), (), s32[]{:S(2)}) async-start(), calls=%async_computation.7 | async-start | bytes 9289728 | tf_op jit(solution)/shard_map/all_gather | solution.py:165
  17.4 636.9 %all-gather.21.cloned.1.call-start = ((), (), s32[]{:S(2)}) async-start(), calls=%async_computation.8 | async-start | bytes 9289728 | tf_op jit(solution)/shard_map/all_gather | solution.py:166
  18.9 729.8 %all-gather.23.cloned.1.call-start = ((), (), s32[]{:S(2)}) async-start(), calls=%async_computation.9 | async-start | bytes 20643840 | tf_op jit(solution)/shard_map/all_gather | solution.py:98
  302.0 804.4 %all-gather.27.cloned.1.call-start = ((), (), s32[]{:S(2)}) async-start(), calls=%async_computation.11 | async-start | bytes 20643840 | tf_op jit(solution)/shard_map/all_gather | solution.py:98
  318.0 836.4 %all-gather.25.cloned.1.call-start = ((), (), s32[]{:S(2)}) async-start(), calls=%async_computation.10 | async-start | bytes 20643840 | tf_op jit(solution)/shard_map/all_gather | solution.py:98
  334.0 912.5 %all-gather.29.cloned.1.call-start = ((), (), s32[]{:S(2)}) async-start(), calls=%async_computation.12 | async-start | bytes 20643840 | tf_op jit(solution)/shard_map/all_gather | solution.py:98
  350.0 1205.6 %all-gather.31.cloned.1.call-start = ((), (), s32[]{:S(2)}) async-start(), calls=%async_computation.13 | async-start | bytes 20643840 | tf_op jit(solution)/shard_map/all_gather | solution.py:98
  390.8 1721.3 %copy-start.98 = (f32[2]{0:T(128)}, f32[2]{0:T(128)S(1)}, u32[]{:S(2)}) copy-start(f32[2]{0:T(128)S(1)} %compare_convert_fusion) | copy-start | bytes 28
  549.9 26.7 copy-start.62
  549.9 26.7 copy-start.79
  549.9 26.7 copy-start.91
  549.9 26.7 copy-start.94
  549.9 26.7 copy-start.117
  549.9 26.7 copy-start.120
  549.9 312.1 %copy-start.76 = (f32[2016]{0:T(1024)}, f32[2016]{0:T(1024)S(1)}, u32[]{:S(2)}) copy-start(f32[2016]{0:T(1024)S(1)} %get-tuple-element.144) | copy-start | bytes 24196
  549.9 312.1 %copy-start.107 = (f32[2016]{0:T(1024)}, f32[2016]{0:T(1024)S(1)}, u32[]{:S(2)}) copy-start(f32[2016]{0:T(1024)S(1)} %get-tuple-element.143) | copy-start | bytes 24196
  682.9 2784.9 %reduce-scatter.27.cloned.1.call-start = ((), (), s32[]{:S(2)}) async-start(), calls=%async_computation.18 | async-start | bytes 20643840
  862.0 23.2 copy-start.65
  862.0 23.2 copy-start.82
  1068.4 125.6 %copy-start.96 = (f32[2016]{0:T(1024)}, f32[2016]{0:T(1024)S(1)}, u32[]{:S(2)}) copy-start(f32[2016]{0:T(1024)S(1)} %get-tuple-element.267) | copy-start | bytes 24196
  1068.4 581.0 %copy-start.70 = (f32[2016]{0:T(1024)}, f32[2016]{0:T(1024)S(1)}, u32[]{:S(2)}) copy-start(f32[2016]{0:T(1024)S(1)} %get-tuple-element.268) | copy-start | bytes 24196
  1154.4 39.6 copy-start.92
  1154.4 39.6 copy-start.118
  1154.4 39.6 copy-start.170
  1246.4 403.7 %copy-start.84 = (f32[2016]{0:T(1024)}, f32[2016]{0:T(1024)S(1)}, u32[]{:S(2)}) copy-start(f32[2016]{0:T(1024)S(1)} %get-tuple-element.266) | copy-start | bytes 24196
  1246.4 403.7 %copy-start.87 = (f32[2016]{0:T(1024)}, f32[2016]{0:T(1024)S(1)}, u32[]{:S(2)}) copy-start(f32[2016]{0:T(1024)S(1)} %get-tuple-element.297) | copy-start | bytes 24196
  1246.4 403.7 %copy-start.112 = (f32[2016]{0:T(1024)}, f32[2016]{0:T(1024)S(1)}, u32[]{:S(2)}) copy-start(f32[2016]{0:T(1024)S(1)} %get-tuple-element.265) | copy-start | bytes 24196
  1246.4 403.7 %copy-start.115 = (f32[2016]{0:T(1024)}, f32[2016]{0:T(1024)S(1)}, u32[]{:S(2)}) copy-start(f32[2016]{0:T(1024)S(1)} %get-tuple-element.298) | copy-start | bytes 24196
  1246.4 39.1 copy-start.110
  1246.5 39.1 copy-start.111
  1246.5 39.0 copy-start.143
  1246.5 39.0 copy-start.144
  1304.9 47.3 copy-start.63
  1304.9 47.3 copy-start.80
  1351.6 297.8 %copy-start.60 = (f32[2016]{0:T(1024)}, f32[2016]{0:T(1024)S(1)}, u32[]{:S(2)}) copy-start(f32[2016]{0:T(1024)S(1)} %get-tuple-element.262) | copy-start | bytes 24196
  1486.1 48.3 copy-start.101
  1486.1 48.3 copy-start.102
  1545.8 188.2 %copy-start.134 = (f32[2,504]{1,0:T(2,128)}, f32[2,504]{1,0:T(2,128)S(1)}, u32[]{:S(2)}) copy-start(f32[2,504]{1,0:T(2,128)S(1)} %fusion.61) | copy-start | bytes 12100
  1549.3 191.2 %copy-start.58 = (f32[2,2016]{1,0:T(2,128)}, f32[2,2016]{1,0:T(2,128)S(1)}, u32[]{:S(2)}) copy-start(f32[2,2016]{1,0:T(2,128)S(1)} %fusion.157) | copy-start | bytes 48388
  1555.6 39.3 copy-start.95
  1555.6 39.3 copy-start.121
  1605.1 44.2 copy-start.66
  1605.1 44.3 copy-start.77
  1605.1 44.3 copy-start.109
  1605.1 45.0 copy-start.52
  1605.1 45.0 copy-start.142
  1713.6 1760.1 %reduce-scatter.21.cloned.1.call-start = ((), (), s32[]{:S(2)}) async-start(), calls=%async_computation.15 | async-start | bytes 20643840
  1970.4 50.7 copy-start.130
  2026.4 54.2 %copy-start.129 = (f32[2,2016]{1,0:T(2,128)S(1)}, f32[2,2016]{1,0:T(2,128)}, u32[]{:S(2)}) copy-start(f32[2,2016]{1,0:T(2,128)} %get-tuple-element.281) | copy-start | bytes 48388
  2095.0 1384.0 %reduce-scatter.25.cloned.1.call-start = ((), (), s32[]{:S(2)}) async-start(), calls=%async_computation.17 | async-start | bytes 20643840
  2112.1 45.1 copy-start.128
  2336.7 1147.9 %reduce-scatter.19.cloned.1.call-start = ((), (), s32[]{:S(2)}) async-start(), calls=%async_computation.14 | async-start | bytes 20643840
  2988.0 93.8 %copy-start.35 = (f32[2,14,14,2016]{3,0,2,1:T(2,128)S(1)}, f32[2,14,14,2016]{3,0,2,1:T(2,128)}, u32[]{:S(2)}) copy-start(f32[2,14,14,2016]{3,0,2,1:T(2,128)} %get-tuple-element.224) | copy-start | bytes 9483268
  3147.5 22.1 copy-start.108
  3169.6 53.6 %copy-start.168 = (f32[2016]{0:T(1024)S(1)}, f32[2016]{0:T(1024)}, u32[]{:S(2)}) copy-start(f32[2016]{0:T(1024)} %get-tuple-element.118) | copy-start | bytes 24196
  3169.6 94.9 %copy-start.122 = (f32[2,2016]{1,0:T(2,128)S(1)}, f32[2,2016]{1,0:T(2,128)}, u32[]{:S(2)}) copy-start(f32[2,2016]{1,0:T(2,128)} %get-tuple-element.282) | copy-start | bytes 48388
  3264.4 22.2 copy-start.163
  3264.4 22.2 copy-start.165
  3264.5 25.0 copy-start.173
  3320.0 251.0 %reduce-scatter.23.cloned.1.call-start = ((), (), s32[]{:S(2)}) async-start(), calls=%async_computation.16 | async-start | bytes 20643840
  3338.2 1604.0 %all-reduce.42.cloned.1.call-start = ((), (), s32[]{:S(2)}) async-start(), calls=%async_computation.19 | async-start | bytes 90832896
  3594.5 1423.2 %all-reduce.44.cloned.1.call-start = ((), (), s32[]{:S(2)}) async-start(), calls=%async_computation.20 | async-start | bytes 6193152 | tf_op jit(solution)/shard_map/psum | solution.py:281
  (130 other events, 747.9 us)
Sparse Core Ops, SparseCore 0:
  13.6 227.0 all-gather.14
  243.5 134.4 all-gather.16
  380.1 140.3 all-gather.18
  523.1 121.3 all-gather.20
  646.0 102.6 all-gather.22
  750.0 105.2 all-gather.26
  856.9 104.4 all-gather.24
  962.9 105.4 all-gather.28
  1070.0 104.7 all-gather.30
  1713.7 125.9 reduce-scatter.26
  2095.1 124.9 reduce-scatter.20
  2336.8 124.6 reduce-scatter.24
  3320.1 123.8 reduce-scatter.18
  3446.5 124.5 reduce-scatter.22
  3594.7 1347.5 all-reduce.41
  4950.3 67.3 all-reduce.43
where the time goes:
time: 5180 us; the launch traced here: 5090 us
  local copies, waits for them, and re-layouts  2130 us (41%)
  waiting for transfers between devices  1680 us (32%)
  blocking collectives  580 us (11%)
  matrix products  389 us (8%)
  other arithmetic  300 us (6%)
    unnamed x22, waiting for transfers between devices  1330 us
    unnamed x402, local copies, waits for them, and re-layouts  486 us
    pad x3, local copies, waits for them, and re-layouts, make_patches(): padded[:, row_tap:row_tap + spanned:stride, col_tap:col_tap + spanned:str...  253 us
    psum x6, blocking collectives, norm_backward(): lax.psum((jnp.sum(grad_masked * scaled, axis=(0, 1, 2)), jnp.sum(grad_mas...  243 us
    psum x6, blocking collectives, norm_forward(): lax.psum((jnp.sum(values * keep_mask, axis=(0, 1, 2)), jnp.sum(values * v...  243 us
    reshape x4, local copies, waits for them, and re-layouts, grouped_backward(): patch_grad.reshape(images_here, side_out, side_out, 9, channels)  240 us
    all_gather x1, waiting for transfers between devices, per_device(): lax.all_gather(pointwise_w.astype(jnp.bfloat16), 'rows', axis=1, tiled=True)  222 us
    all_gather x5, local copies, waits for them, and re-layouts, pointwise_forward(): full_weight = lax.all_gather(column, 'chan', axis=1, tiled=True)  196 us
  transfers between devices with their start and end apart: 16, of which 5 were waited for; matrix products, arithmetic and copies ran while one was open for 52% of the time, Pallas kernels for 0%

commit v1 on v0

v1 whole, which is shorter than its diff:
```python
import functools

import jax
import jax.numpy as jnp
import numpy as np
from jax import lax
from jax.experimental import pallas as pl
from jax.experimental.pallas import tpu as pltpu
from jax.sharding import PartitionSpec as P

GROUPS = 36
GW = 56

highest = lax.Precision.HIGHEST
epsilon = 1e-05
momentum_rate = 0.9
learn_rate = 20.0
norm_rate = 0.1
weight_decay = 5e-05
trust_coef = 0.02
bf16 = jnp.bfloat16
f32 = jnp.float32
AXES = ("rows", "chan")
NT = (((1,), (1,)), ((), ()))
NN = (((1,), (0,)), ((), ()))


def round_up(value, step):
    return (value + step - 1) // step * step


class Wire:
    def __init__(self, rows, chan):
        self.rows, self.chan = rows, chan
        self.row = lax.axis_index("rows")
        self.col = lax.axis_index("chan")
        self.deep = [
            (dr << 1, dc << 2) for dc in range(max(1, chan // 4)) for dr in range(rows // 2)
        ]
        place_r, place_c = [], []
        core = self.col & 1
        for dc in range(2):
            for second in range(2):
                for first in range(2):
                    for dr, dk in self.deep:
                        source = core ^ dc
                        dy = jnp.where(source == 0, first, second)
                        dx = jnp.where(source == 0, second, first)
                        place_r.append(self.row ^ dr ^ dy)
                        place_c.append(self.col ^ dk ^ dc ^ (dx << 1))
        self.place = jnp.stack([jnp.stack(place_r), jnp.stack(place_c)]).astype(jnp.int32)
        count = rows * chan
        self.groups = [list(range(core, count, 2)) for core in range(2)]
        index = jnp.arange(count // 2, dtype=jnp.int32) * 2
        halves = [index + core, index + (1 - core)]
        self.place_half = jnp.concatenate([jnp.stack([h // chan, h % chan]) for h in halves], axis=1)

    def swap(self, value, mask):
        pairs = []
        for device in range(self.rows * self.chan):
            r, c = device // self.chan, device % self.chan
            dr, dc = mask(c & 1) if callable(mask) else mask
            pairs.append((device, (r ^ dr) * self.chan + (c ^ dc)))
        return lax.ppermute(value, AXES, pairs)

    def first(self, value):
        return self.swap(value, lambda core: (1, 0) if core == 0 else (0, 2))

    def second(self, value):
        return self.swap(value, lambda core: (0, 2) if core == 0 else (1, 0))

    def core(self, value):
        return self.swap(value, (0, 1))

    def tree(self, parts):
        while len(parts) > 1:
            parts = [parts[i] + parts[i + 1] for i in range(0, len(parts), 2)]
        return parts[0]

    def sum_planes(self, value):
        for masks in ([(1, 0), (0, 2), (1, 2)], self.deep[1:]):
            value = self.tree([value] + [self.swap(value, mask) for mask in masks])
        return value

    def gather_half(self, shard):
        return lax.all_gather(shard, AXES, axis_index_groups=self.groups)

    def sum_chips(self, value):
        count = self.rows * self.chan
        groups = [list(range(core, count, 2)) for core in range(2)]
        copies = jnp.broadcast_to(value[None], (count // 2,) + value.shape)
        copies = lax.all_to_all(copies, AXES, 0, 0, axis_index_groups=groups, tiled=True)
        return jnp.sum(copies, axis=0)

    def trade(self, values):
        return lax.all_to_all(values, AXES, 0, 0, tiled=True)


class Gather:
    def __init__(self, wire, shard):
        self.wire, self.items, self.stage = wire, [shard], 0

    def go(self, items):
        wire, self.items = self.wire, items
        if self.stage == 0:
            self.pending = [wire.swap(items[0], mask) for mask in wire.deep[1:]]
        else:
            step = (None, wire.first, wire.second, wire.core)[self.stage]
            self.pending = [step(item) for item in items]

    def arrive(self, arrived):
        if self.stage == 0:
            self.items = [jnp.stack(self.items + arrived)]
        elif self.stage == 1:
            self.items = [jnp.concatenate(self.items + arrived)]
        else:
            self.items = self.items + arrived
        self.stage += 1


class Scatter:
    def __init__(self, wire, blocks=None, sent=None):
        self.wire, self.stage = wire, 1
        if blocks is None:
            self.items = [sent]
            return
        half = blocks.shape[0] // 2
        self.keep, self.items = blocks[:half], [blocks[half:]]
        if 2 * half == wire.rows * wire.chan:
            self.stage = 0

    def go(self, items):
        wire, self.items = self.wire, items
        if self.stage < 3:
            step = (wire.core, wire.second, wire.first)[self.stage]
            self.pending = [step(items[0])]
        else:
            self.pending = [wire.swap(item, mask) for item, mask in zip(items, wire.deep[1:])]

    def arrive(self, arrived):
        def add(a, b):
            return (a.astype(f32) + b.astype(f32)).astype(bf16)

        if self.stage < 2:
            half = self.keep.shape[0] // 2
            self.items = [add(self.keep[half:], arrived[0][half:])]
            self.keep = add(self.keep[:half], arrived[0][:half])
        elif self.stage == 2:
            parts = [add(self.keep[i], arrived[0][i]) for i in range(len(self.wire.deep))]
            self.keep, self.items = parts[0], parts[1:]
        else:
            self.total = self.wire.tree([part.astype(f32) for part in [self.keep] + arrived])
        self.stage += 1


class Pair:
    def __init__(self, wire, value):
        self.wire, self.items = wire, [value]

    def go(self, items):
        self.items, self.pending = items, [self.wire.core(items[0])]

    def arrive(self, arrived):
        self.items = self.items + arrived


def hook(value, wait=(), go=()):
    value, arrived, items = lax.optimization_barrier(
        (value, [flow.pending for flow in wait], [f.items for f in go if f not in wait])
    )
    for flow, got in zip(wait, arrived):
        flow.arrive(got)
    items = iter(items)
    for flow in go:
        flow.go(flow.items if flow in wait else next(items))
    return value


def widen(value, blocks, size):
    value = value.reshape(value.shape[:-1] + (blocks, -1))
    value = jnp.pad(value, [(0, 0)] * (value.ndim - 1) + [(0, size - value.shape[-1])])
    return value.reshape(value.shape[:-2] + (blocks * size,))


def narrow(value, blocks, size):
    value = value.reshape(value.shape[:-1] + (blocks, -1))[..., :size]
    return value.reshape(value.shape[:-2] + (blocks * size,))


def sigmoid(value):
    return 0.5 * jnp.tanh(0.5 * value) + 0.5


def silu(value):
    half = 0.5 * value
    return half * jnp.tanh(half) + half


def silu_slope(value):
    gate = sigmoid(value)
    return gate * (1.0 + value * (1.0 - gate))


def fold(value):
    return jnp.sum(value.reshape(value.shape[0] // 8, 8, value.shape[1]), axis=0)


def down(value):
    return jnp.sum(value, axis=0, keepdims=True)


def stats_of(sums, number):
    average = sums[0:1] / number
    return average, lax.rsqrt(sums[1:2] / number - average * average + epsilon)


def forward_scale(sums, norm, j, number):
    average, inverse = stats_of(sums, number)
    a = norm[j : j + 1] * inverse
    return a, norm[7 + j : 8 + j] - average * a


def backward_scale(sums, back, norm, j, number):
    average, inverse = stats_of(sums, number)
    a = norm[j : j + 1] * inverse
    c = -a * inverse * back[0:1] / number
    return a, c, -a * back[1:2] / number - c * average


def sds(shape, dtype):
    return jax.ShapeDtypeStruct(shape, dtype)


ANY = pl.BlockSpec(memory_space=pl.ANY)
VM = pl.BlockSpec(memory_space=pltpu.VMEM)
SM = pl.BlockSpec(memory_space=pltpu.SMEM)


def call(body, outs, args, specs, out_specs=None, scratch=(), grid=(), flops=0, moved=0):
    return pl.pallas_call(
        body,
        out_shape=outs,
        grid=grid,
        in_specs=specs,
        out_specs=out_specs if out_specs is not None else [VM] * len(outs),
        scratch_shapes=list(scratch),
        compiler_params=pltpu.CompilerParams(
            vmem_limit_bytes=60 * 1024 * 1024,
            dimension_semantics=("arbitrary",) * len(grid) if grid else None,
        ),
        cost_estimate=pl.CostEstimate(flops=flops, bytes_accessed=moved, transcendentals=0),
    )(*args)


def load_weight(place, pieces, dest, sem, start):
    height, width = pieces[0].shape[1:]
    count = pieces[0].shape[0]
    if not start:
        pltpu.make_async_copy(dest, dest, sem).wait()
        return
    for k, piece in enumerate(pieces):
        for i in range(count):
            p = k * count + i
            r = pl.multiple_of(place[0, p] * height, height)
            c = pl.multiple_of(place[1, p] * width, width)
            pltpu.make_async_copy(
                piece.at[i], dest.at[pl.ds(r, height), pl.ds(c, width)], sem
            ).start()


def lane_tiles(full, step, body):
    @pl.loop(0, full // step)
    def _(i):
        body(pl.ds(pl.multiple_of(i * step, step), step))


def point_kernel(place, x_ref, *rest):
    pieces, (out_ref, sums_ref, w_ref, sem) = rest[:-4], rest[-4:]

    @pl.when(pl.program_id(0) == 0)
    def _():
        load_weight(place, pieces, w_ref, sem, True)
        sums_ref[...] = jnp.zeros_like(sums_ref)
        load_weight(place, pieces, w_ref, sem, False)

    x = x_ref[...].reshape(-1, x_ref.shape[-1])

    def chunk(lanes):
        result = jnp.dot(x, w_ref[:, lanes], preferred_element_type=f32).astype(bf16)
        out_ref[..., lanes] = result.reshape(out_ref.shape[:-1] + (result.shape[1],))
        wide = result.astype(f32)
        sums_ref[0:1, lanes] += down(fold(wide))
        sums_ref[1:2, lanes] += down(fold(wide * wide))

    lane_tiles(w_ref.shape[1], 512, chunk)


def point(place, x, pieces, planes):
    slots, _, rows, full = x.shape
    spec = pl.BlockSpec((slots, 1, rows, full), lambda i: (0, i, 0, 0))
    outs = [sds((slots, planes, rows, full), bf16), sds((2, full), f32)]
    return call(
        point_kernel,
        outs,
        (place, x, *pieces),
        [SM, spec] + [ANY] * len(pieces),
        [spec, pl.BlockSpec((2, full), lambda i: (0, 0))],
        [pltpu.VMEM((full, full), bf16), pltpu.SemaphoreType.DMA],
        (planes,),
        2 * slots * planes * rows * full * full,
        full * full * 2 + 4 * slots * planes * rows * full,
    )


def weight_kernel(order, *refs):
    pairs, out_ref = refs[:-1], refs[-1]
    count, height, width = out_ref.shape
    full = pairs[0].shape[1]
    down_blocks = full // height

    @pl.loop(0, down_blocks)
    def _(r):
        rows = pl.ds(pl.multiple_of(r * height, height), height)
        turned = [x[:, rows].T for x in pairs[0::2]]
        for k in range(count // down_blocks):
            spot = order[0, r * (count // down_blocks) + k]
            c = order[1, r * (count // down_blocks) + k]
            across = pl.ds(pl.multiple_of(c * width, width), width)
            block = 0.0
            for xt, g in zip(turned, pairs[1::2]):
                block = block + jnp.dot(xt, g[:, across], preferred_element_type=f32)
            out_ref[spot] = block.astype(bf16)


def weight_grad(order, pairs, height, width):
    rows, full = pairs[0].shape
    count = order.shape[1]
    return call(
        weight_kernel,
        [sds((count, height, width), bf16)],
        (order, *pairs),
        [SM] + [VM] * len(pairs),
        flops=len(pairs) * rows * height * width * count,
        moved=count * height * width * 2 + 2 * rows * full * len(pairs),
    )[0]


def plane_weight_kernel(order, x0_ref, x1_ref, g0_ref, g1_ref, out_ref):
    count, height, width = out_ref.shape
    slots, _, rows, full = x0_ref.shape
    down_blocks = full // height
    each = count // down_blocks

    @pl.loop(0, down_blocks)
    def _(r):
        lanes = pl.ds(pl.multiple_of(r * height, height), height)
        turned = [x[:, 0, :, lanes].reshape(slots * rows, height).T for x in (x0_ref, x1_ref)]
        for k in range(each):
            across = pl.ds(pl.multiple_of(order[1, r * each + k] * width, width), width)
            block = 0.0
            for xt, g in zip(turned, (g0_ref, g1_ref)):
                block = block + jnp.dot(xt, g[:, across], preferred_element_type=f32)
            out_ref[order[0, r * each + k]] = block.astype(bf16)


def plane_weight_grad(order, x_pair, g_pair, height, width):
    slots, _, rows, full = x_pair[0].shape
    count = order.shape[1]
    x_spec = pl.BlockSpec((slots, 1, rows, full), lambda i: (0, 0, 0, 0))
    g_spec = pl.BlockSpec((slots * rows, full), lambda i: (0, 0))
    return call(
        plane_weight_kernel,
        [sds((count, height, width), bf16)],
        (order, *x_pair, *g_pair),
        [SM, x_spec, x_spec, g_spec, g_spec],
        [pl.BlockSpec((count, height, width), lambda i: (0, 0, 0))],
        (),
        (1,),
        4 * slots * rows * height * width * count,
        count * height * width * 2 + 8 * slots * rows * full,
    )[0]


def entry_weight_kernel(spots, x0_ref, x1_ref, g0_ref, g1_ref, out_ref):
    planes, rows, height = x0_ref.shape[1], x0_ref.shape[2], x0_ref.shape[3]
    depth = x0_ref.shape[0] * rows
    block = 0.0
    for x_ref, g_ref in ((x0_ref, g0_ref), (x1_ref, g1_ref)):
        for k in range(planes):
            x = x_ref[:, k].reshape(depth, height)
            block = block + jnp.dot(g_ref[k, :, 0:depth], x, preferred_element_type=f32)
    out_ref[0] = block.T.astype(bf16)


def entry_weight(spots, x_pair, g_pair, height, width):
    slots, planes, rows, full = x_pair[0].shape
    count, deep = spots.shape[1], g_pair[0].shape[2]
    x_spec = pl.BlockSpec((slots, planes, rows, height), lambda i, at: (0, 0, 0, at[0, i]))
    g_spec = pl.BlockSpec((planes, width, deep), lambda i, at: (0, at[1, i], 0))
    return pl.pallas_call(
        entry_weight_kernel,
        out_shape=[sds((count, height, width), bf16)],
        grid_spec=pltpu.PrefetchScalarGridSpec(
            num_scalar_prefetch=1,
            grid=(count,),
            in_specs=[x_spec, x_spec, g_spec, g_spec],
            out_specs=[pl.BlockSpec((1, height, width), lambda i, at: (i, 0, 0))],
        ),
        compiler_params=pltpu.CompilerParams(
            vmem_limit_bytes=60 * 1024 * 1024, dimension_semantics=("arbitrary",)
        ),
        cost_estimate=pl.CostEstimate(
            flops=4 * slots * planes * rows * height * width * count,
            bytes_accessed=4 * x_pair[0].size,
            transcendentals=0,
        ),
    )(spots, *x_pair, *g_pair)[0]


def prepare_kernel(count, select, x_ref, out_ref, rows_ref, *, blocks):
    _, high, side_in, channels = x_ref.shape
    block = channels // blocks
    lanes = out_ref.shape[-1] // blocks
    pad = rows_ref.shape[0] // high

    @pl.when((pl.program_id(0) == 0) & (pl.program_id(1) == 0))
    def _():
        rows_ref[...] = jnp.zeros_like(rows_ref)

    live = pl.program_id(0) < count[0]
    for h in range(high):
        value = x_ref[0, h]
        rows_ref[h * pad : h * pad + side_in, :] = jnp.where(live, value, jnp.zeros_like(value))
    sorted_rows = jnp.dot(select[...], rows_ref[...], preferred_element_type=f32)
    shape = out_ref.shape[1:-1]
    for r in range(blocks):
        part = sorted_rows[:, r * block : (r + 1) * block]
        part = jnp.concatenate(
            [part, jnp.zeros((part.shape[0], lanes - block), f32)], axis=1
        )
        out_ref[0, :, :, :, :, r * lanes : (r + 1) * lanes] = part.astype(bf16).reshape(
            shape + (lanes,)
        )


def parity_select(high, pad, side_in, wide):
    out = np.zeros((high * 2 * wide, high * pad), np.float32)
    for h in range(high):
        for w in range(side_in):
            target = (((h % 2) * 2 + w % 2) * (high // 2) + h // 2) * wide + w // 2
            out[target, h * pad + w] = 1.0
    return out


def prepare(count, images, blocks, lanes, wide):
    slots, side_in, _, channels = images.shape
    side, high, pad = side_in // 2, 4, 32
    select = jnp.asarray(parity_select(high, pad, side_in, wide), bf16)
    full = blocks * lanes
    return call(
        functools.partial(prepare_kernel, blocks=blocks),
        [sds((slots, 2, 2, side, wide, full), bf16)],
        (count, select, images),
        [
            SM,
            pl.BlockSpec(select.shape, lambda n, q: (0, 0)),
            pl.BlockSpec((1, high, side_in, channels), lambda n, q: (n, q, 0, 0)),
        ],
        [pl.BlockSpec((1, 2, 2, high // 2, wide, full), lambda n, q: (n, 0, 0, q, 0, 0))],
        [pltpu.VMEM((high * pad, channels), bf16)],
        (slots, side_in // high),
        moved=images.size * 4,
    )[0]


def restore_kernel(select, even_ref, odd_ref, out_ref, *, blocks):
    _, high, side_in, channels = out_ref.shape
    block = channels // blocks
    full = even_ref.shape[-1]
    lanes = full // blocks
    value = jnp.concatenate([ref[0].reshape(-1, full) for ref in (even_ref, odd_ref)], axis=0)
    rows = jnp.dot(select[...], value, preferred_element_type=f32)
    pad = rows.shape[0] // high
    joined = jnp.concatenate(
        [rows[:, r * lanes : r * lanes + block] for r in range(blocks)], axis=1
    ).astype(bf16)
    for h in range(high):
        out_ref[0, h] = joined[h * pad : h * pad + side_in]


def restore(even, odd, blocks, channels):
    slots, _, side, wide, full = even.shape
    side_in, high, pad = 2 * side, 4, 32
    select = jnp.asarray(parity_select(high, pad, side_in, wide).T, bf16)
    spec = pl.BlockSpec((1, 2, high // 2, wide, full), lambda n, q: (n, 0, q, 0, 0))
    return call(
        functools.partial(restore_kernel, blocks=blocks),
        [sds((slots, side_in, side_in, channels), bf16)],
        (select, even, odd),
        [pl.BlockSpec(select.shape, lambda n, q: (0, 0)), spec, spec],
        [pl.BlockSpec((1, high, side_in, channels), lambda n, q: (n, q, 0, 0))],
        (),
        (slots, side_in // high),
        moved=even.size * 8,
    )[0]


def widen_kernel(v_ref, out_ref, *, blocks):
    _, high, side, channels = v_ref.shape
    block = channels // blocks
    lanes = out_ref.shape[-1] // blocks
    wide = out_ref.shape[2]
    for h in range(high):
        value = v_ref[0, h].astype(f32)
        value = jnp.concatenate([value, jnp.zeros((wide - side, channels), f32)], axis=0)
        for r in range(blocks):
            part = value[:, r * block : (r + 1) * block]
            part = jnp.concatenate([part, jnp.zeros((wide, lanes - block), f32)], axis=1)
            out_ref[0, h, :, r * lanes : (r + 1) * lanes] = part.astype(bf16)


def widen_image(value, blocks, lanes, wide):
    slots, side, _, channels = value.shape
    full = blocks * lanes
    return call(
        functools.partial(widen_kernel, blocks=blocks),
        [sds((slots, side, wide, full), bf16)],
        (value,),
        [pl.BlockSpec((1, 2, side, channels), lambda n, q: (n, q, 0, 0))],
        [pl.BlockSpec((1, 2, wide, full), lambda n, q: (n, q, 0, 0))],
        (),
        (slots, side // 2),
        moved=value.size * 4,
    )[0]


def narrow_kernel(v_ref, out_ref, *, blocks):
    _, high, side, channels = out_ref.shape
    block = channels // blocks
    lanes = v_ref.shape[-1] // blocks
    for h in range(high):
        value = v_ref[0, h].astype(f32)
        joined = jnp.concatenate(
            [value[:, r * lanes : r * lanes + block] for r in range(blocks)], axis=1
        )
        out_ref[0, h] = joined[:side].astype(bf16)


def narrow_image(value, blocks, channels):
    slots, side, wide, full = value.shape
    return call(
        functools.partial(narrow_kernel, blocks=blocks),
        [sds((slots, side, side, channels), bf16)],
        (value,),
        [pl.BlockSpec((1, 2, wide, full), lambda n, q: (n, q, 0, 0))],
        [pl.BlockSpec((1, 2, side, channels), lambda n, q: (n, q, 0, 0))],
        (),
        (slots, side // 2),
        moved=value.size * 4,
    )[0]


def dense_kernel(w_ref, place_ref, same_ref, out_ref):
    for t in range(w_ref.shape[0]):
        spread = jnp.dot(place_ref[...], w_ref[t], preferred_element_type=f32)
        out_ref[t, 0] = (spread * same_ref[...].astype(f32)).astype(bf16)


def dense_grouped(weight, place, same):
    nine, part, full = weight.shape
    tile = same.shape[0]
    tiles = full // tile
    return call(
        dense_kernel,
        [sds((nine, tiles, tile, tile), bf16)],
        (weight, place, same),
        [
            pl.BlockSpec((nine, part, tile), lambda j: (0, 0, j)),
            pl.BlockSpec(place.shape, lambda j: (0, 0)),
            pl.BlockSpec(same.shape, lambda j: (0, 0)),
        ],
        [pl.BlockSpec((nine, 1, tile, tile), lambda j: (0, j, 0, 0))],
        (),
        (tiles,),
        moved=nine * full * tile * 2,
    )[0]


def tap_views(stride):
    views = []
    for a in range(3):
        for b in range(3):
            if stride == 1:
                views.append((0, 0, a - 1, b - 1))
            else:
                views.append((int(a != 1), int(b != 1), -int(a == 0), -int(b == 0)))
    return views


def fill_planes(store, a_ref, scale, offset, keep_ref, wide, stride, slope_ref=None):
    slots, planes, rows, tile = a_ref.shape
    gap = rows + wide

    @pl.when(pl.program_id(0) == 0)
    def _():
        zero = jnp.zeros(store.shape[:1] + (wide, tile), bf16)
        for n in range(slots + 1):
            if n * gap < store.shape[1]:
                store[:, n * gap : n * gap + wide, :] = zero

    def chunk(lanes):
        a, b = scale[:, lanes], offset[:, lanes]
        for n in range(slots):
            mask = keep_ref[n * rows : (n + 1) * rows, :]
            for k in range(planes):
                y = (a_ref[n, k, :, lanes].astype(f32) * a + b) * mask
                half = 0.5 * y
                t = jnp.tanh(half)
                h = half * t + half
                if slope_ref is not None:
                    slope_ref[n, k, :, lanes] = (0.5 * t + 0.5) * (1.0 + half * (1.0 - t))
                span = slice(n * gap + wide, n * gap + wide + rows)
                if stride == 1:
                    store[0, span, lanes] = pltpu.roll(h, 1, 0).astype(bf16)
                    store[1, span, lanes] = h.astype(bf16)
                    store[2, span, lanes] = pltpu.roll(h, rows - 1, 0).astype(bf16)
                else:
                    hp, wp = k // 2, k % 2
                    store[hp * 3 + wp, span, lanes] = h.astype(bf16)
                    if wp:
                        store[hp * 3 + 2, span, lanes] = pltpu.roll(h, 1, 0).astype(bf16)

    for lane in range(0, tile, 128):
        chunk(slice(lane, lane + 128))


def view_of(store, tap, stride, wide, span):
    hp, wp, dy, dx = tap
    which = dx + 1 if stride == 1 else hp * 3 + wp - dx
    start = wide + dy * wide
    return store[which, start : start + span, :]


def grouped_kernel(number, sums_ref, norm_ref, keep_ref, a_ref, dense_ref, out_ref, osum_ref,
                   store, scales, *, j, stride, wide, which):
    slots, planes, rows, tile = a_ref.shape
    scale, offset = forward_scale(sums_ref[...], norm_ref[...], j, number[which])
    scales[0:1], scales[1:2] = scale, offset
    fill_planes(store, a_ref, scales.at[0:1], scales.at[1:2], keep_ref, wide, stride)
    span = slots * rows + (slots - 1) * wide
    total = None
    for t, tap in enumerate(tap_views(stride)):
        part = jnp.dot(
            view_of(store, tap, stride, wide, span), dense_ref[t, 0], preferred_element_type=f32
        )
        total = part if total is None else total + part
    first = second = 0.0
    for n in range(slots):
        start = n * (rows + wide)
        mask = jnp.concatenate([keep_ref[n * rows : (n + 1) * rows, :]] * (tile // 128), axis=1)
        value = total[start : start + rows] * mask
        out_ref[n * rows : (n + 1) * rows, :] = value.astype(bf16)
        first = first + down(fold(value))
        second = second + down(fold(value * value))
    osum_ref[0:1], osum_ref[1:2] = first, second


def lane_block(shape, tile):
    zeros = (0,) * (len(shape) - 1)
    return pl.BlockSpec(shape[:-1] + (tile,), lambda i: zeros + (i,))


def plane_rows(stride):
    return 3 if stride == 1 else 6


def grouped_forward(number, sums, norm, keep, a, dense, j, stride, wide, which):
    slots, planes, rows, full = a.shape
    tile = dense.shape[-1]
    height = wide + slots * (rows + wide)
    return call(
        functools.partial(grouped_kernel, j=j, stride=stride, wide=wide, which=which),
        [sds((slots * rows, full), bf16), sds((2, full), f32)],
        (number, sums, norm, keep, a, dense),
        [
            SM,
            lane_block(sums.shape, tile),
            lane_block(norm.shape, tile),
            pl.BlockSpec(keep.shape, lambda i: (0, 0)),
            lane_block(a.shape, tile),
            pl.BlockSpec((9, 1, tile, tile), lambda i: (0, i, 0, 0)),
        ],
        [lane_block((slots * rows, full), tile), lane_block((2, full), tile)],
        [pltpu.VMEM((plane_rows(stride), height, tile), bf16), pltpu.VMEM((2, tile), f32)],
        (full // tile,),
        18 * slots * rows * full * tile,
        dense.size * 2 + a.size * 2,
    )


def grouped_back_kernel(number, sums_ref, norm_ref, keep_ref, a_ref, dense_ref, g_ref, c_ref,
                        csum_ref, cback_ref, place_ref, same_ref, dv_ref, back_ref, kernel_ref,
                        store, scales, grads, slope, *, j, stride, wide, which):
    slots, planes, rows, tile = a_ref.shape
    gap = rows + wide
    number_in, number_out = number[which], number[1]
    scale, offset = forward_scale(sums_ref[...], norm_ref[...], j, number_in)
    scales[0:1], scales[1:2] = scale, offset
    fill_planes(store, a_ref, scales.at[0:1], scales.at[1:2], keep_ref, wide, stride, slope)
    ga, gc, gb = backward_scale(csum_ref[...], cback_ref[...], norm_ref[...], j + 1, number_out)
    scales[2:3], scales[3:4], scales[4:5] = ga, gc, gb

    @pl.when(pl.program_id(0) == 0)
    def _():
        for n in range(slots + 1):
            grads[:, n * gap : n * gap + wide, :] = jnp.zeros((3, wide, tile), bf16)

    for lane in range(0, tile, 128):
        lanes = slice(lane, lane + 128)
        pa, pc, pb = scales[2:3, lanes], scales[3:4, lanes], scales[4:5, lanes]
        for n in range(slots):
            span = slice(n * rows, (n + 1) * rows)
            g, c = g_ref[span, lanes].astype(f32), c_ref[span, lanes].astype(f32)
            dc = (g * pa + c * pc + pb) * keep_ref[span, :]
            to = slice(n * gap + wide, n * gap + wide + rows)
            grads[1, to, lanes] = dc.astype(bf16)
            grads[2, to, lanes] = pltpu.roll(dc, rows - 1, 0).astype(bf16)
            if stride == 1:
                grads[0, to, lanes] = pltpu.roll(dc, 1, 0).astype(bf16)
    span = slots * rows + (slots - 1) * wide
    fields = {}
    for t, (hp, wp, dy, dx) in enumerate(tap_views(stride)):
        start = wide - dy * wide
        part = lax.dot_general(
            grads[1 - dx, start : start + span, :], dense_ref[t, 0], NT,
            preferred_element_type=f32,
        )
        key = hp * 2 + wp
        fields[key] = part if key not in fields else fields[key] + part
    first = second = 0.0
    average, inverse = stats_of(sums_ref[...], number_in)
    for n in range(slots):
        mask = jnp.concatenate([keep_ref[n * rows : (n + 1) * rows, :]] * (tile // 128), axis=1)
        for k in range(planes):
            dv = fields[k][n * gap : n * gap + rows] * slope[n, k] * mask
            dv_ref[n, k] = dv.astype(dv_ref.dtype)
            first = first + down(fold(dv * ((a_ref[n, k].astype(f32) - average) * inverse)))
            second = second + down(fold(dv))
    back_ref[0:1], back_ref[1:2] = first, second
    flat = grads[1, wide : wide + span, :].T
    for t, tap in enumerate(tap_views(stride)):
        dense_grad = jnp.dot(
            flat, view_of(store, tap, stride, wide, span), preferred_element_type=f32
        )
        kept = (dense_grad * same_ref[...].astype(f32)).astype(bf16)
        kernel_ref[t] = lax.dot_general(
            place_ref[...], kept, NT, preferred_element_type=f32
        ).astype(bf16)


def grouped_backward(number, sums, norm, keep, a, dense, g, c, csum, cback, place_t, same, j,
                     stride, wide, which, dtype):
    slots, planes, rows, full = a.shape
    tile = dense.shape[-1]
    part = place_t.shape[0]
    height = wide + slots * (rows + wide)
    flat = (slots * rows, full)
    return call(
        functools.partial(grouped_back_kernel, j=j, stride=stride, wide=wide, which=which),
        [sds(a.shape, dtype), sds((2, full), f32), sds((9, part, full), bf16)],
        (number, sums, norm, keep, a, dense, g, c, csum, cback, place_t, same),
        [
            SM,
            lane_block(sums.shape, tile),
            lane_block(norm.shape, tile),
            pl.BlockSpec(keep.shape, lambda i: (0, 0)),
            lane_block(a.shape, tile),
            pl.BlockSpec((9, 1, tile, tile), lambda i: (0, i, 0, 0)),
            lane_block(flat, tile),
            lane_block(flat, tile),
            lane_block(csum.shape, tile),
            lane_block(cback.shape, tile),
            pl.BlockSpec(place_t.shape, lambda i: (0, 0)),
            pl.BlockSpec(same.shape, lambda i: (0, 0)),
        ],
        [lane_block(a.shape, tile), lane_block((2, full), tile), lane_block((9, part, full), tile)],
        [
            pltpu.VMEM((plane_rows(stride), height, tile), bf16),
            pltpu.VMEM((8, tile), f32),
            pltpu.VMEM((3, height, tile), bf16),
            pltpu.VMEM((slots, planes, rows, tile), f32),
        ],
        (full // tile,),
        54 * slots * rows * full * tile,
        dense.size * 2 + a.size * 2,
    )


def split_dot(value, weight, dims):
    high = value.astype(bf16).astype(f32)
    rows = jnp.concatenate([high, value - high], axis=0).astype(bf16)
    result = lax.dot_general(rows, weight, dims, preferred_element_type=f32)
    return result[:8] + result[8:]


def excite_kernel(number, place, sums_ref, norm_ref, keep_ref, c_ref, sq_ref, ex_ref, *rest,
                  j, slots, pixels):
    pieces, rest = rest[:-11], rest[-11:]
    e_ref, a_ref, osum_ref, pool_ref, gate_ref, pre_ref, q_ref, w_ref, sem, hold, scales = rest
    load_weight(place, pieces, w_ref, sem, True)
    scales[0:1], scales[1:2] = forward_scale(sums_ref[...], norm_ref[...], j, number[1])
    rows, full = c_ref.shape
    each = rows // slots
    pool_ref[...] = jnp.zeros_like(pool_ref)

    def pass_one(lanes):
        a, b = scales[0:1, lanes], scales[1:2, lanes]
        for n in range(slots):
            span = slice(n * each, (n + 1) * each)
            h = silu((c_ref[span, lanes].astype(f32) * a + b) * keep_ref[span, :])
            hold[span, lanes] = h
            pool_ref[n : n + 1, lanes] = down(fold(h)) * (1.0 / pixels)

    lane_tiles(full, 128, pass_one)
    pre = split_dot(pool_ref[...], sq_ref[...], NT)
    q = silu(pre)
    pre_ref[...], q_ref[...] = pre, q
    gate_ref[...] = sigmoid(split_dot(q, ex_ref[...], NN))

    def pass_two(lanes):
        for n in range(slots):
            span = slice(n * each, (n + 1) * each)
            e_ref[span, lanes] = (hold[span, lanes] * gate_ref[n : n + 1, lanes]).astype(bf16)

    lane_tiles(full, 128, pass_two)
    load_weight(place, pieces, w_ref, sem, False)
    matmul_sums(e_ref, w_ref, a_ref, osum_ref)


def matmul_sums(x_ref, w_ref, out_ref, sums_ref):
    def chunk(lanes):
        result = jnp.dot(x_ref[...], w_ref[:, lanes], preferred_element_type=f32).astype(bf16)
        out_ref[:, lanes] = result
        wide = result.astype(f32)
        sums_ref[0:1, lanes] = down(fold(wide))
        sums_ref[1:2, lanes] = down(fold(wide * wide))

    lane_tiles(w_ref.shape[1], 512, chunk)


def weight_scratch(full):
    return [pltpu.VMEM((full, full), bf16), pltpu.SemaphoreType.DMA]


def excite_forward(number, place, sums, norm, keep, c, sq, ex, pieces, j, slots, pixels):
    rows, full = c.shape
    se = sq.shape[0]
    return call(
        functools.partial(excite_kernel, j=j, slots=slots, pixels=pixels),
        [
            sds((rows, full), bf16),
            sds((rows, full), bf16),
            sds((2, full), f32),
            sds((8, full), f32),
            sds((8, full), f32),
            sds((8, se), f32),
            sds((8, se), f32),
        ],
        (number, place, sums, norm, keep, c, sq, ex, *pieces),
        [SM, SM, VM, VM, VM, VM, VM, VM] + [ANY] * len(pieces),
        scratch=weight_scratch(full)
        + [pltpu.VMEM((rows, full), f32), pltpu.VMEM((8, full), f32)],
        flops=2 * rows * full * full,
        moved=full * full * 2 + rows * full * 8,
    )


def join_kernel(number, place, sum2_ref, sum3_ref, norm_ref, keep_ref, a_ref, s_ref, *rest):
    pieces, rest = rest[:-7], rest[-7:]
    z_ref, m_ref, out_ref, osum_ref, w_ref, sem, scales = rest
    load_weight(place, pieces, w_ref, sem, True)
    scales[0:1], scales[1:2] = forward_scale(sum2_ref[...], norm_ref[...], 2, number[1])
    scales[2:3], scales[3:4] = forward_scale(sum3_ref[...], norm_ref[...], 3, number[1])

    def chunk(lanes):
        z = (
            a_ref[:, lanes].astype(f32) * scales[0:1, lanes]
            + s_ref[:, lanes].astype(f32) * scales[2:3, lanes]
            + (scales[1:2, lanes] + scales[3:4, lanes])
        ) * keep_ref[...]
        z_ref[:, lanes] = z.astype(bf16)
        m_ref[:, lanes] = silu(z).astype(bf16)

    lane_tiles(a_ref.shape[1], 128, chunk)
    load_weight(place, pieces, w_ref, sem, False)
    matmul_sums(m_ref, w_ref, out_ref, osum_ref)


def join_forward(number, place, sum2, sum3, norm, keep, a, s, pieces):
    rows, full = a.shape
    return call(
        join_kernel,
        [
            sds((rows, full), bf16),
            sds((rows, full), bf16),
            sds((rows, full), bf16),
            sds((2, full), f32),
        ],
        (number, place, sum2, sum3, norm, keep, a, s, *pieces),
        [SM, SM, VM, VM, VM, VM, VM, VM] + [ANY] * len(pieces),
        scratch=weight_scratch(full) + [pltpu.VMEM((8, full), f32)],
        flops=2 * rows * full * full,
        moved=full * full * 2 + rows * full * 8,
    )


def turn_kernel(number, sums_ref, norm_ref, keep_ref, a_ref, z_ref, g_ref, act_ref, d_ref,
                back_ref, scales):
    scales[0:1], scales[1:2] = forward_scale(sums_ref[...], norm_ref[...], 6, number[1])
    scales[2:3], scales[3:4] = stats_of(sums_ref[...], number[1])

    def chunk(lanes):
        a = a_ref[:, lanes].astype(f32)
        z = (a * scales[0:1, lanes] + scales[1:2, lanes]) * keep_ref[...]
        z = z + silu(z_ref[:, lanes].astype(f32))
        half = 0.5 * z
        t = jnp.tanh(half)
        act_ref[:, lanes] = (half * t + half).astype(bf16)
        d = g_ref[:, lanes].astype(f32) * ((0.5 * t + 0.5) * (1.0 + half * (1.0 - t)))
        d_ref[:, lanes] = d.astype(bf16)
        dz = d * keep_ref[...]
        scaled = (a - scales[2:3, lanes]) * scales[3:4, lanes]
        back_ref[0:1, lanes] = down(fold(dz * scaled))
        back_ref[1:2, lanes] = down(fold(dz))

    lane_tiles(a_ref.shape[1], 128, chunk)


def turn(number, sums, norm, keep, a, z, g):
    rows, full = a.shape
    return call(
        turn_kernel,
        [sds((rows, full), bf16), sds((rows, full), bf16), sds((2, full), f32)],
        (number, sums, norm, keep, a, z, g),
        [SM] + [VM] * 6,
        scratch=[pltpu.VMEM((8, full), f32)],
        moved=rows * full * 14,
    )


def norm_back_pass(d_ref, a_ref, keep_ref, scales, out_ref):
    def chunk(lanes):
        out_ref[:, lanes] = (
            (
                d_ref[:, lanes].astype(f32) * scales[0:1, lanes]
                + a_ref[:, lanes].astype(f32) * scales[1:2, lanes]
                + scales[2:3, lanes]
            )
            * keep_ref[...]
        ).astype(bf16)

    lane_tiles(a_ref.shape[1], 128, chunk)


def excite_back_kernel(number, place, sums_ref, back_ref, csum_ref, norm_ref, keep_ref, d_ref,
                       a_ref, c_ref, sq_ref, ex_ref, gate_ref, pre_ref, *rest, j, slots, pixels):
    pieces, rest = rest[:-10], rest[-10:]
    da_ref, du_ref, oback_ref, dgate_ref, dpre_ref, w_ref, sem, hold, scales, pool = rest
    load_weight(place, pieces, w_ref, sem, True)
    rows, full = a_ref.shape
    each = rows // slots
    scales[0:1], scales[1:2], scales[2:3] = backward_scale(
        sums_ref[...], back_ref[...], norm_ref[...], j + 1, number[1]
    )
    scales[3:4], scales[4:5] = forward_scale(csum_ref[...], norm_ref[...], j, number[1])
    scales[5:6], scales[6:7] = stats_of(csum_ref[...], number[1])
    norm_back_pass(d_ref, a_ref, keep_ref, scales, da_ref)
    dgate_ref[...] = jnp.zeros_like(dgate_ref)
    load_weight(place, pieces, w_ref, sem, False)

    def chunk(lanes):
        de = lax.dot_general(da_ref[...], w_ref[lanes, :], NT, preferred_element_type=f32)
        hold[:, lanes] = de

    lane_tiles(full, 512, chunk)

    def gates(lanes):
        a, b = scales[3:4, lanes], scales[4:5, lanes]
        for n in range(slots):
            span = slice(n * each, (n + 1) * each)
            h = silu((c_ref[span, lanes].astype(f32) * a + b) * keep_ref[span, :])
            dgate_ref[n : n + 1, lanes] = down(fold(hold[span, lanes] * h))

    lane_tiles(full, 128, gates)
    gate = gate_ref[...]
    d_gate = dgate_ref[...] * gate * (1.0 - gate)
    dgate_ref[...] = d_gate
    d_pre = split_dot(d_gate, ex_ref[...], NT) * silu_slope(pre_ref[...])
    dpre_ref[...] = d_pre
    pool[...] = split_dot(d_pre, sq_ref[...], NN) * (1.0 / pixels)

    def finish(lanes):
        a, b = scales[3:4, lanes], scales[4:5, lanes]
        first = second = 0.0
        for n in range(slots):
            span = slice(n * each, (n + 1) * each)
            c = c_ref[span, lanes].astype(f32)
            slope = silu_slope((c * a + b) * keep_ref[span, :])
            dh = hold[span, lanes] * gate_ref[n : n + 1, lanes] + pool[n : n + 1, lanes]
            du = dh * slope * keep_ref[span, :]
            du_ref[span, lanes] = du.astype(bf16)
            first = first + down(fold(du * ((c - scales[5:6, lanes]) * scales[6:7, lanes])))
            second = second + down(fold(du))
        oback_ref[0:1, lanes], oback_ref[1:2, lanes] = first, second

    lane_tiles(full, 128, finish)


def excite_backward(number, place, sums, back, csum, norm, keep, d, a, c, sq, ex, gate, pre,
                    pieces, j, slots, pixels):
    rows, full = a.shape
    se = sq.shape[0]
    return call(
        functools.partial(excite_back_kernel, j=j, slots=slots, pixels=pixels),
        [
            sds((rows, full), bf16),
            sds((rows, full), bf16),
            sds((2, full), f32),
            sds((8, full), f32),
            sds((8, se), f32),
        ],
        (number, place, sums, back, csum, norm, keep, d, a, c, sq, ex, gate, pre, *pieces),
        [SM, SM] + [VM] * 12 + [ANY] * len(pieces),
        scratch=weight_scratch(full)
        + [
            pltpu.VMEM((rows, full), f32),
            pltpu.VMEM((8, full), f32),
            pltpu.VMEM((8, full), f32),
        ],
        flops=2 * rows * full * full,
        moved=full * full * 2 + rows * full * 16,
    )


def join_back_kernel(number, place, sums_ref, back_ref, sum2_ref, sum3_ref, norm_ref, keep_ref,
                     d_ref, a_ref, skip_ref, z_ref, a3_ref, s_ref, *rest):
    pieces, rest = rest[:-7], rest[-7:]
    da_ref, dz_ref, oback_ref, w_ref, sem, scales, hold = rest
    load_weight(place, pieces, w_ref, sem, True)
    scales[0:1], scales[1:2], scales[2:3] = backward_scale(
        sums_ref[...], back_ref[...], norm_ref[...], 4, number[1]
    )
    scales[3:4], scales[4:5] = stats_of(sum2_ref[...], number[1])
    scales[5:6], scales[6:7] = stats_of(sum3_ref[...], number[1])
    norm_back_pass(d_ref, a_ref, keep_ref, scales, da_ref)
    load_weight(place, pieces, w_ref, sem, False)

    def chunk(lanes):
        dm = lax.dot_general(da_ref[...], w_ref[lanes, :], NT, preferred_element_type=f32)
        hold[:, lanes] = dm

    lane_tiles(a_ref.shape[1], 512, chunk)

    def finish(lanes):
        dm = hold[:, lanes] + skip_ref[:, lanes].astype(f32)
        dz = dm * silu_slope(z_ref[:, lanes].astype(f32)) * keep_ref[...]
        dz_ref[:, lanes] = dz.astype(bf16)
        scaled2 = (a3_ref[:, lanes].astype(f32) - scales[3:4, lanes]) * scales[4:5, lanes]
        scaled3 = (s_ref[:, lanes].astype(f32) - scales[5:6, lanes]) * scales[6:7, lanes]
        oback_ref[0:1, lanes] = down(fold(dz * scaled2))
        oback_ref[1:2, lanes] = down(fold(dz))
        oback_ref[2:3, lanes] = down(fold(dz * scaled3))

    lane_tiles(a_ref.shape[1], 128, finish)


def join_backward(number, place, sums, back, sum2, sum3, norm, keep, d, a, skip, z, a3, s,
                  pieces):
    rows, full = a.shape
    return call(
        join_back_kernel,
        [sds((rows, full), bf16), sds((rows, full), bf16), sds((3, full), f32)],
        (number, place, sums, back, sum2, sum3, norm, keep, d, a, skip, z, a3, s, *pieces),
        [SM, SM] + [VM] * 12 + [ANY] * len(pieces),
        scratch=weight_scratch(full)
        + [pltpu.VMEM((8, full), f32), pltpu.VMEM((rows, full), f32)],
        flops=2 * rows * full * full,
        moved=full * full * 2 + rows * full * 20,
    )


def side_kernel(number, place, sums_ref, back_ref, norm_ref, keep_ref, d_ref, a_ref, *rest):
    pieces, rest = rest[:-5], rest[-5:]
    da_ref, dx_ref, w_ref, sem, scales = rest
    load_weight(place, pieces, w_ref, sem, True)
    scales[0:1], scales[1:2], scales[2:3] = backward_scale(
        sums_ref[...], back_ref[...], norm_ref[...], 3, number[1]
    )
    norm_back_pass(d_ref, a_ref, keep_ref, scales, da_ref)
    load_weight(place, pieces, w_ref, sem, False)

    def chunk(lanes):
        dx_ref[:, lanes] = lax.dot_general(
            da_ref[...], w_ref[lanes, :], NT, preferred_element_type=f32
        ).astype(bf16)

    lane_tiles(a_ref.shape[1], 512, chunk)


def side_backward(number, place, sums, back, norm, keep, d, a, pieces):
    rows, full = a.shape
    return call(
        side_kernel,
        [sds((rows, full), bf16), sds((rows, full), bf16)],
        (number, place, sums, back, norm, keep, d, a, *pieces),
        [SM, SM] + [VM] * 6 + [ANY] * len(pieces),
        scratch=weight_scratch(full) + [pltpu.VMEM((8, full), f32)],
        flops=2 * rows * full * full,
        moved=full * full * 2 + rows * full * 12,
    )


def entry_norm_kernel(number, sums_ref, back_ref, norm_ref, keep_ref, d_ref, a_ref, da_ref,
                      turn_ref, scales):
    scales[0:1], scales[1:2], scales[2:3] = backward_scale(
        sums_ref[...], back_ref[...], norm_ref[...], 0, number[0]
    )
    slots, _, rows, full = d_ref.shape

    def chunk(lanes):
        d = d_ref[:, :, :, lanes].reshape(slots * rows, 128).astype(f32)
        a = a_ref[:, :, :, lanes].reshape(slots * rows, 128).astype(f32)
        da = (d * scales[0:1, lanes] + a * scales[1:2, lanes] + scales[2:3, lanes]) * keep_ref[...]
        da = da.astype(bf16)
        da_ref[:, :, :, lanes] = da.reshape(slots, 1, rows, 128)
        spare = jnp.zeros((128, turn_ref.shape[2] - slots * rows), bf16)
        turn_ref[0, lanes, :] = jnp.concatenate([da.T, spare], axis=1)

    lane_tiles(full, 128, chunk)


def entry_norm(number, sums, back, norm, keep, d, a):
    slots, planes, rows, full = a.shape
    spec = pl.BlockSpec((slots, 1, rows, full), lambda i: (0, i, 0, 0))
    whole = lambda v: pl.BlockSpec(v.shape, lambda i: (0, 0))
    deep = round_up(slots * rows, 128)
    return call(
        entry_norm_kernel,
        [sds(a.shape, bf16), sds((planes, full, deep), bf16)],
        (number, sums, back, norm, keep, d, a),
        [SM, whole(sums), whole(back), whole(norm), whole(keep), spec, spec],
        [spec, pl.BlockSpec((1, full, deep), lambda i: (i, 0, 0))],
        [pltpu.VMEM((8, full), f32)],
        (planes,),
        moved=a.size * 8,
    )


def entry_kernel(place, da_ref, side_ref, *rest, odd):
    pieces, rest = rest[:-3], rest[-3:]
    dx_ref, w_ref, sem = rest

    @pl.when(pl.program_id(0) == 0)
    def _():
        load_weight(place, pieces, w_ref, sem, True)
        load_weight(place, pieces, w_ref, sem, False)

    slots, _, rows, full = da_ref.shape
    da = da_ref[...].reshape(-1, full)
    extra = (pl.program_id(0) == 0).astype(f32)

    def chunk(lanes):
        dx = lax.dot_general(da, w_ref[lanes, :], NT, preferred_element_type=f32)
        if not odd:
            dx = dx + side_ref[:, lanes].astype(f32) * extra
        dx_ref[..., lanes] = dx.astype(bf16).reshape(dx_ref.shape[:-1] + (dx.shape[1],))

    lane_tiles(full, 512, chunk)


def entry_backward(place, da, side, pieces, odd):
    slots, planes, rows, full = da.shape
    half = planes // 2
    read = pl.BlockSpec((slots, 1, rows, full), lambda i: (0, i + half * odd, 0, 0))
    spec = pl.BlockSpec((slots, 1, rows, full), lambda i: (0, i, 0, 0))
    return call(
        functools.partial(entry_kernel, odd=odd),
        [sds((slots, half, rows, full), bf16)],
        (place, da, side, *pieces),
        [SM, read, pl.BlockSpec(side.shape, lambda i: (0, 0))] + [ANY] * len(pieces),
        [spec],
        weight_scratch(full),
        (half,),
        da.size * full,
        full * full * 2 + da.size * 2,
    )[0]


def collect_kernel(place, *refs):
    pieces, (sq_ref, ex_ref, gr_ref, more_ref) = refs[:-4], refs[-4:]
    each = sq_ref.shape[1]
    count, groups, sixteen, lanes = pieces[0].shape
    last = 2 * each + 9
    for k, piece in enumerate(pieces):
        for i in range(count):
            p = k * count + i
            across = pl.ds(pl.multiple_of(place[0, p] * lanes, lanes), lanes)
            c = place[1, p]
            sq_ref[c, :, :, across] = piece[i, 0:each]
            ex_ref[c, :, :, across] = piece[i, each : 2 * each]
            part = pl.ds(pl.multiple_of(c * sixteen, sixteen), sixteen)
            gr_ref[:, part, across] = piece[i, 2 * each : last]
            if groups > last:
                more_ref[:, :, across] = piece[i, last:]


def collect(place, pieces, chan, se_groups, full):
    _, groups, sixteen, _ = pieces[0].shape
    more = max(1, groups - 2 * se_groups - 9)
    return call(
        collect_kernel,
        [
            sds((chan, se_groups, sixteen, full), bf16),
            sds((chan, se_groups, sixteen, full), bf16),
            sds((9, chan * sixteen, full), bf16),
            sds((more, sixteen, full), bf16),
        ],
        (place, *pieces),
        [SM] + [VM] * len(pieces),
        moved=12 * 1024 * 1024,
    )


def deal_kernel(place, value_ref, out_ref):
    count, _, height, lanes = out_ref.shape
    for p in range(count):
        across = pl.ds(pl.multiple_of(place[0, p] * lanes, lanes), lanes)
        part = pl.ds(pl.multiple_of(place[1, p] * height, height), height)
        out_ref[p] = value_ref[:, part, across]


def deal(place, value, height, lanes):
    nine, part, full = value.shape
    count = part * full // (height * lanes)
    return call(
        deal_kernel,
        [sds((count, nine, height, lanes), bf16)],
        (place, value),
        [SM, VM],
        moved=value.size * 4,
    )[0]


def per_device(
    images,
    counts,
    out_grad,
    pointwise_w,
    grouped_w,
    squeeze_w,
    excite_w,
    norm_params,
    pointwise_m,
    grouped_m,
    squeeze_m,
    excite_m,
    norm_m,
):
    rows, chan = lax.axis_size("rows"), lax.axis_size("chan")
    wire = Wire(rows, chan)
    slots, side_in = images.shape[0], images.shape[1]
    side = out_grad.shape[1]
    wide = round_up(side, 16)
    block = norm_params.shape[2]
    lanes = round_up(block, 128)
    full = rows * lanes
    per_chan = rows // chan
    se = squeeze_w.shape[2]
    se_block = se // chan
    se_wide = 512 // chan
    se_full = chan * se_wide
    gw_part = GW // chan
    gw_wide = round_up(gw_part, 16)
    image = side * wide
    pixels = side * side

    index = wire.row * chan + wire.col
    own_count = lax.dynamic_index_in_dim(counts, index, keepdims=False)
    live = jnp.arange(slots, dtype=jnp.int32) < own_count
    valid = jnp.arange(wide, dtype=jnp.int32) < side
    keep = live[:, None, None] & valid[None, None, :]
    keep = jnp.broadcast_to(keep, (slots, side, wide)).reshape(slots * image, 1)
    keep = jnp.broadcast_to(keep.astype(f32), (slots * image, 128))
    live_total = jnp.sum(counts).astype(f32)
    number = jnp.stack([live_total * side_in * side_in, live_total * pixels])
    place = wire.place
    spots = jnp.arange(rows * chan, dtype=jnp.int32)

    def order_of(wanted):
        key = (place[0] * chan + place[1])[None]
        spot = jnp.sum(jnp.where(key == wanted[:, None], spots[None], 0), axis=1)
        return jnp.stack([spot, wanted % chan]).astype(jnp.int32)

    order_all = order_of(spots)
    order_core = order_of(spots[: rows * chan // 2] * 2 + (wire.col & 1))

    shards = widen(pointwise_w.astype(bf16), per_chan, lanes)
    shards = jnp.pad(shards, ((0, 0), (0, lanes - block), (0, 0)))

    def part_of(value, axis, size):
        return lax.dynamic_slice_in_dim(value, wire.col * size, size, axis)

    squeeze_part = jnp.swapaxes(part_of(squeeze_w, 2, se_block), 1, 2)
    excite_part = part_of(excite_w, 1, se_block)
    grouped_part = part_of(grouped_w, 2, gw_part)
    pad_lane = (0, lanes - block)
    squeeze_part = jnp.pad(squeeze_part, ((0, 0), (0, se_wide - se_block), pad_lane))
    excite_part = jnp.pad(excite_part, ((0, 0), (0, se_wide - se_block), pad_lane))
    grouped_part = jnp.pad(grouped_part, ((0, 0), (0, 0), (0, gw_wide - gw_part), pad_lane))
    small_shard = jnp.concatenate(
        [squeeze_part, excite_part, grouped_part.reshape(2, 9 * gw_wide, lanes)], axis=1
    ).astype(bf16)
    small_shard = small_shard.reshape(2, -1, 16, lanes)
    norm_rest = jnp.pad(norm_params.reshape(14, block), ((0, 2), pad_lane))
    norm_terms = []
    for _ in range(3):
        term = lax.reduce_precision(norm_rest, 8, 7)
        norm_terms.append(term.astype(bf16))
        norm_rest = norm_rest - term
    small_shard1 = jnp.concatenate([small_shard[0], jnp.stack(norm_terms)])

    fetch0, fetch1, fetch3 = [Gather(wire, shards[k]) for k in (0, 1, 3)]
    small2 = Gather(wire, small_shard[1])
    index_all = jnp.arange(rows * chan, dtype=jnp.int32)
    place_all = jnp.stack([index_all // chan, index_all % chan])

    def unpack(where, pieces):
        sq, ex, gr, extra = collect(where, pieces, chan, se_wide // 16, full)
        return (
            sq.reshape(se_full, full),
            ex.reshape(se_full, full),
            gr.reshape(9, chan * gw_wide, full),
            extra,
        )

    tile = 9 * GW // block * lanes
    position = np.arange(tile)
    inside = position % lanes
    channel = position // lanes * block + inside
    good = inside < block
    group = np.where(good, channel // GW, -1)
    within = channel % GW
    slot = within // gw_part * gw_wide + within % gw_part
    spread = (slot[:, None] == np.arange(chan * gw_wide)[None]) & good[:, None]
    same = jnp.asarray((group[:, None] == group[None]) & good[:, None], bf16)
    spread_t, spread = jnp.asarray(spread.T, bf16), jnp.asarray(spread, bf16)

    width = per_chan * lanes

    def both_cores(x_own, x_other, g_own, g_other):
        return weight_grad(order_core, (x_own, g_own, x_other, g_other), lanes, width)

    def sum_all(value, go=(), wait=(), beside=None, uses=()):
        value = value + wire.core(value)
        value, uses = hook((value, uses), go=go)
        if beside is None:
            value = wire.sum_planes(value)
            return hook(value, wait=wait) if wait else value
        value = wire.sum_chips(value)
        return hook((value, beside(*uses)), wait=wait)

    def vectors_of(pool, dgate, q, dpre):
        split = [
            v[:slots].reshape(slots, rows, lanes).transpose(1, 0, 2) for v in (pool, dgate)
        ]
        whole = [jnp.broadcast_to(v[:slots], (rows,) + v[:slots].shape) for v in (q, dpre)]
        sent = jnp.concatenate(split + whole, axis=2)
        sent = jnp.repeat(sent, chan, axis=0)
        return sent

    small1 = [lax.all_gather(small_shard1, AXES)]
    fetch0.go(fetch0.items)
    x = prepare(own_count[None], images, rows, lanes, wide).reshape(slots, 4, image, full)
    x, out_grad = hook((x, out_grad), (fetch0,), (fetch0,))
    gout = widen_image(out_grad, rows, lanes, wide).reshape(slots * image, full)
    x, gout = hook((x, gout), (fetch0,), (fetch0, fetch1))
    x = hook(x, (fetch0, fetch1), (fetch0, fetch1))
    place1, x = lax.optimization_barrier((place_all, x))
    sq1, ex1, gr1, norm_terms = unpack(place1, small1)
    dense1 = dense_grouped(gr1, spread, same)
    x, dense1, shard2 = hook((x, dense1, shards[2]), (fetch0, fetch1), (fetch1, fetch3))
    weight2 = Pair(wire, wire.gather_half(shard2))
    a1, sum0 = point(place, x, fetch0.items, 4)
    sum0 = hook(sum0, (fetch1, fetch3))
    sum0 = sum_all(sum0, go=(fetch1,), wait=(fetch1,))
    norm = jnp.sum(norm_terms.astype(f32), axis=0)[:14]
    sum0, shard4 = hook((sum0, shards[4]), go=(fetch3, small2))
    weight4 = Pair(wire, wire.gather_half(shard4))
    place_half = wire.place_half
    c1, sum1 = grouped_forward(number, sum0, norm, keep, a1, dense1, 0, 2, wide, 0)
    sum1 = hook(sum1, (fetch3, small2))
    sum1 = sum_all(sum1)
    sum1 = hook(sum1, go=(small2, fetch3, weight2))
    e1, a3, sum2, pool1, gate1, pre1, q1 = excite_forward(
        number, place, sum1, norm, keep, c1, sq1, ex1, fetch1.items, 1, slots, pixels
    )
    side_x, sum2 = hook((x, sum2), (weight2,))
    s1, sum3 = point(place_half, side_x, weight2.items, 1)
    s1 = s1.reshape(slots * image, full)
    sums = hook(jnp.concatenate([sum2, sum3]), (small2, fetch3))
    sums = sum_all(sums, go=(fetch3,), wait=(fetch3,))
    e1_pair = Pair(wire, e1)
    sums = hook(sums, go=(small2, e1_pair))
    sum2, sum3 = sums[:2], sums[2:]
    z1, m16, a4, sum4 = join_forward(
        number, place, sum2, sum3, norm, keep, a3, s1, fetch3.items
    )
    sum4 = hook(sum4, (small2, e1_pair))
    sum4 = sum4 + wire.core(sum4)
    sum4 = hook(sum4, go=(small2,))
    place2 = hook(place, (small2,))
    sq2, ex2, gr2, _ = unpack(place2, small2.items)
    dense2 = dense_grouped(gr2, spread, same)
    m16_pair = Pair(wire, m16)
    sum4, dense2 = hook((wire.sum_chips(sum4), dense2), go=(m16_pair, weight4))
    a4 = a4.reshape(slots, 1, image, full)
    c2, sum5 = grouped_forward(number, sum4, norm, keep, a4, dense2, 4, 1, wide, 1)
    sum5 = hook(sum5, (m16_pair, weight4))
    sum5 = sum_all(sum5)
    e2, a5, sum6, pool2, gate2, pre2, q2 = excite_forward(
        number, place_half, sum5, norm, keep, c2, sq2, ex2, weight4.items, 5, slots, pixels
    )
    sum6 = sum_all(sum6)
    e2_pair = Pair(wire, e2)
    sum6 = hook(sum6, go=(e2_pair,))
    act, d2, back6 = turn(number, sum6, norm, keep, a5, z1, gout)
    back6 = hook(back6, (e2_pair,))
    back6, activations = sum_all(
        back6,
        beside=lambda wide_act: narrow_image(
            wide_act.reshape(slots, side, wide, full), rows, images.shape[3]
        ),
        uses=(act,),
    )
    x_pair = Pair(wire, x)
    back6 = hook(back6, go=(x_pair,))
    da5, du2, back5, dgate2, dpre2 = excite_backward(
        number, place_half, sum6, back6, sum5, norm, keep, d2, a5, c2, sq2, ex2, gate2, pre2,
        weight4.items, 5, slots, pixels
    )
    back5 = hook(back5, (x_pair,))
    da5_pair = Pair(wire, da5)
    back5 = sum_all(back5, go=(da5_pair,), wait=(da5_pair,))
    dv2, back4, kernel2 = grouped_backward(
        number, sum4, norm, keep, a4, dense2, du2, c2, sum5, back5, spread_t, same, 4, 1, wide,
        1, bf16
    )
    back4, grad4 = sum_all(back4, beside=both_cores, uses=e2_pair.items + da5_pair.items)
    flow4 = Scatter(wire, grad4)
    back4 = hook(back4, go=(flow4,))
    flat4 = a4.reshape(slots * image, full)
    da4, dz1, back23 = join_backward(
        number, place, sum4, back4, sum2, sum3, norm, keep, dv2.reshape(slots * image, full),
        flat4, d2, z1, a3, s1, fetch3.items
    )
    back23 = hook(back23, (flow4,))
    da4_pair = Pair(wire, da4)
    back23 = sum_all(back23, go=(da4_pair,), wait=(da4_pair,))
    flow6 = Scatter(wire, deal(place, kernel2, gw_wide, lanes))
    back23 = hook(back23, go=(flow4, flow6))
    back2, back3 = back23[:2], jnp.stack([back23[2], back23[1]])
    da3, du1, back1, dgate1, dpre1 = excite_backward(
        number, place, sum2, back2, sum1, norm, keep, dz1, a3, c1, sq1, ex1, gate1, pre1,
        fetch1.items, 1, slots, pixels
    )
    back1 = hook(back1, (flow4, flow6))
    da3_pair = Pair(wire, da3)
    back1, grad3 = sum_all(
        back1,
        go=(da3_pair,),
        wait=(da3_pair,),
        beside=both_cores,
        uses=m16_pair.items + da4_pair.items,
    )
    flow3 = Scatter(wire, grad3)
    back1 = hook(back1, go=(flow3, flow6, flow4))
    grad1 = both_cores(*e1_pair.items, *da3_pair.items)
    flow1 = Scatter(wire, grad1)
    back1, pool1 = hook((back1, pool1), go=(flow1,))
    sent = [vectors_of(pool1, dgate1, q1, dpre1), vectors_of(pool2, dgate2, q2, dpre2)]
    vectors = wire.trade(jnp.concatenate(sent, axis=2)).reshape(rows * chan * slots, -1)
    dv1, back0, kernel1 = grouped_backward(
        number, sum0, norm, keep, a1, dense1, du1, c1, sum1, back1, spread_t, same, 0, 2, wide,
        0, bf16
    )
    back0, vectors = hook((back0, vectors), (flow3, flow6, flow4, flow1))
    back0, ((ds1, dside), deal1) = sum_all(
        back0,
        beside=lambda dz, k: (
            side_backward(number, place_half, sum3, back3, norm, keep, dz, s1, weight2.items),
            deal(place, k, gw_wide, lanes),
        ),
        uses=(dz1, kernel1),
    )
    ds1_pair, flow7 = Pair(wire, ds1), Scatter(wire, deal1)
    back0 = hook(back0, go=(ds1_pair, flow3, flow1, flow6, flow7))
    da1, da1_turned = entry_norm(number, sum0, back0, norm, keep, dv1, a1)
    da1_pair = Pair(wire, da1_turned)
    da1, dside = hook((da1, dside), (ds1_pair, flow3, flow6, flow7), (da1_pair, flow7, flow3))
    grad2 = plane_weight_grad(order_core, x_pair.items, ds1_pair.items, lanes, width)
    flow2 = Scatter(wire, grad2)
    da1, dside = hook((da1, dside), (flow1, flow7), (flow2,))
    dx_even = entry_backward(place, da1, dside, fetch0.items, 0)
    dx_even, dside, place = hook((dx_even, dside, place), (da1_pair, flow3), (flow1, flow7))
    quarter = rows * chan // 4
    sent0 = entry_weight(place[:, quarter : 2 * quarter], x_pair.items, da1_pair.items, lanes, width)
    flow0 = Scatter(wire, sent=sent0)
    place0 = hook(place, (flow2, flow7), (flow0, flow2))
    flow0.keep = entry_weight(place0[:, :quarter], x_pair.items, da1_pair.items, lanes, width)
    _, da1 = lax.optimization_barrier((flow0.keep, da1))
    dx_odd = entry_backward(place, da1, dside, fetch0.items, 1)
    dx_odd, dx_even = hook((dx_odd, dx_even), (flow0, flow1, flow2), (flow0, flow2))
    shape = (slots, 2, side, wide, full)
    input_grad = restore(dx_even.reshape(shape), dx_odd.reshape(shape), rows, images.shape[3])
    _, (vectors, totals) = hook(
        (input_grad, (vectors, [flow.total for flow in (flow1, flow3, flow4)])),
        (flow0, flow2),
        (flow0, flow6, flow7),
    )
    flow1.total, flow3.total, flow4.total = totals
    vectors = hook(vectors, (flow6, flow7))
    half = vectors.shape[1] // 2
    vectors1, vectors2 = vectors[:, :half], vectors[:, half:]
    vectors1 = hook(vectors1, (flow0,))

    grad_pointwise = jnp.stack(
        [flow.total for flow in (flow0, flow1, flow2, flow3, flow4)]
    )
    grad_pointwise = narrow(grad_pointwise[:, :block], per_chan, block)
    kernel_part = jnp.stack([flow7.total, flow6.total])[:, :, :gw_part, :block]
    parts = [kernel_part] + [wire.swap(kernel_part, (0, d)) for d in range(1, chan)]
    bit = 1
    while bit < chan:
        high = (wire.col & bit) != 0
        parts = [jnp.where(high, parts[i ^ bit], parts[i]) for i in range(chan)]
        bit *= 2
    grad_grouped = jnp.concatenate(parts, axis=2)

    vectors = jnp.stack([vectors1, vectors2])
    pooled_all, gate_all = vectors[:, :, :block], vectors[:, :, lanes : lanes + block]
    q_all = narrow(vectors[:, :, 2 * lanes : 2 * lanes + se_full], chan, se_block)
    pre_all = narrow(vectors[:, :, 2 * lanes + se_full :], chan, se_block)
    grad_squeeze = jnp.einsum("lnk,lns->lks", pooled_all, pre_all, precision=highest)
    grad_excite = jnp.einsum("lns,lnk->lsk", q_all, gate_all, precision=highest)
    backs = [back0, back1, back2, back3, back4, back5, back6]
    grad_norm = jnp.stack([jnp.stack([b[0] for b in backs]), jnp.stack([b[1] for b in backs])])
    grad_norm = lax.dynamic_slice_in_dim(grad_norm, wire.row * lanes, lanes, 2)[:, :, :block]

    def squares(tensor, weighting):
        return weighting * jnp.sum(tensor * tensor, axis=tuple(range(1, tensor.ndim)))

    leader = (wire.col == 0).astype(f32)
    weight_list = (pointwise_w, grouped_w, squeeze_w, excite_w)
    grad_list = (grad_pointwise, grad_grouped, grad_squeeze, grad_excite)
    scales = (1.0, leader, leader, leader)
    terms = [squares(t, s) for t, s in zip(weight_list + grad_list, scales + scales)]
    terms = jnp.concatenate(terms)
    terms = wire.sum_planes(terms + wire.core(terms))
    layer_norms = jnp.sqrt(terms).reshape(2, 11)
    weight_norms, grad_norms = layer_norms[0], layer_norms[1]
    ratio = trust_coef * weight_norms / (grad_norms + weight_decay * weight_norms)

    def lars_step(weight, moment, gradient, ratios):
        scaled_rate = ratios.reshape((-1,) + (1,) * (weight.ndim - 1))
        moment_new = momentum_rate * moment + learn_rate * scaled_rate * (
            gradient + weight_decay * weight
        )
        return (moment_new, weight - moment_new)

    moment_pointwise, new_pointwise = lars_step(
        pointwise_w, pointwise_m, grad_pointwise, ratio[0:5]
    )
    moment_grouped, new_grouped = lars_step(grouped_w, grouped_m, grad_grouped, ratio[5:7])
    moment_squeeze, new_squeeze = lars_step(squeeze_w, squeeze_m, grad_squeeze, ratio[7:9])
    moment_excite, new_excite = lars_step(excite_w, excite_m, grad_excite, ratio[9:11])
    moment_norm = momentum_rate * norm_m + norm_rate * grad_norm
    new_norm = norm_params - moment_norm
    return (
        activations,
        input_grad,
        layer_norms,
        grad_pointwise,
        grad_grouped,
        grad_squeeze,
        grad_excite,
        grad_norm,
        moment_pointwise,
        moment_grouped,
        moment_squeeze,
        moment_excite,
        moment_norm,
        new_pointwise,
        new_grouped,
        new_squeeze,
        new_excite,
        new_norm,
    )


def solution(mesh):
    image = P(("rows", "chan"), None, None, None)
    point = P(None, "rows", "chan")
    grouped = P(None, None, None, "rows")
    squeeze = P(None, "rows", None)
    excite = P(None, None, "rows")
    weights = (point, grouped, squeeze, excite, excite)
    return jax.shard_map(
        per_device,
        mesh=mesh,
        in_specs=(image, P(), image) + weights + weights,
        out_specs=(image, image, P()) + weights + weights + weights,
        check_vma=False,
    )
```

time: 5180 us -> 1100 us (0.21); the launches traced: 5090 us -> 1090 us
  local copies, waits for them, and re-layouts: 2130 us -> 112 us
  waiting for transfers between devices: 1680 us -> 181 us
  blocking collectives: 580 us -> 16 us
  Pallas kernels: 0 us -> 466 us
  matrix products: 389 us -> 6.9 us
  other arithmetic: 300 us -> 104 us
  starting transfers between devices: 0.83 us -> 188 us
    unnamed x22 -> x3, waiting for transfers between devices: 1330 us -> 0.05 us
    psum x13 -> x0, blocking collectives: 526 us -> none  [the longest x6 243 us: norm_backward(): lax.psum((jnp.sum(grad_masked * scaled, axis=(0, 1, 2)), jnp.sum(grad_mas...]
    pallas_call x0 -> x33, Pallas kernels: none -> 466 us  [the longest x31 434 us: call(): pl.pallas_call(body, out_shape=outs, grid=grid, in_specs=specs, out_specs...]
    pad x5 -> x2, local copies, waits for them, and re-layouts: 438 us -> 0.26 us  [the longest x1 0.23 us: widen(): jnp.pad(value, [(0, 0)] * (value.ndim - 1) + [(0, size - value.shape[-1])])]
    unnamed x402 -> x222, local copies, waits for them, and re-layouts: 486 us -> 53.3 us
    dot_general x33 -> x2, matrix products: 389 us -> 6.9 us  [the longest x1 3.45 us: per_device(): grad_excite = jnp.einsum('lns,lnk->lsk', q_all, gate_all, precision=highest)]
    slice x15 -> x24, local copies, waits for them, and re-layouts: 365 us -> 25.7 us  [the longest x6 14.4 us: __init__(): self.keep, self.items = (blocks[:half], [blocks[half:]])]
    reshape x12 -> x11, local copies, waits for them, and re-layouts: 292 us -> 16.9 us  [the longest x3 6.97 us: narrow(): value = value.reshape(value.shape[:-1] + (blocks, -1))[..., :size]]
  transfers between devices with their start and end apart: 16 -> 148, of which waited for: 5 -> 61; matrix products, arithmetic and copies ran while one was open for 52% -> 15% of each run, Pallas kernels for 0% -> 37%
where the time goes in v1:
time: 1100 us; the launch traced here: 1090 us
  Pallas kernels  466 us (42%)
  starting transfers between devices  188 us (17%)
  waiting for transfers between devices  181 us (16%)
  local copies, waits for them, and re-layouts  112 us (10%)
  other arithmetic  104 us (9%)
  between operations  16.5 us (2%)
  blocking collectives  16 us (1%)
    pallas_call x31, Pallas kernels, call(): pl.pallas_call(body, out_shape=outs, grid=grid, in_specs=specs, out_specs...  434 us
    ppermute x140, waiting for transfers between devices, swap(): return lax.ppermute(value, AXES, pairs)  168 us
    ppermute x140, starting transfers between devices, swap(): return lax.ppermute(value, AXES, pairs)  165 us
    unnamed x222, local copies, waits for them, and re-layouts  53.3 us
    convert_element_type x16, other arithmetic, add(): return (a.astype(f32) + b.astype(f32)).astype(bf16)  37.5 us
    pallas_call x2, Pallas kernels, entry_weight(): pl.pallas_call(entry_weight_kernel, out_shape=[sds((count, height, width)...  32.4 us
  transfers between devices with their start and end apart: 148, of which 61 were waited for; matrix products, arithmetic and copies ran while one was open for 15% of the time, Pallas kernels for 37%

profile of v1, /device:TPU:0, one launch (start us, length us, event | category | flops | bytes accessed | tf_op | source)
XLA Modules:
  0.0 1091.2 jit_solution(9228867961176160765)
XLA Ops:
  24.6 9.1 copy.127.x_ref
  34.3 13.7 %shard_map.313 = bf16[2,2,2,14,16,2048]{5,4,3,2,1,0:T(8,128)(2,1)} custom-call(s32[1]{0:T(128)} %dynamic_slice.16.count, bf16[128,128]{1,0:T(8,128)(2,1)} %constant.147.clone.select, bf16[2,28,28,2016]{3,2,1,0:T(8,128)(2,1)} %copy.127.x_ref), custom_call_target="tpu_custom_call" | custom-call | bytes 12644352 | tf_op jit(solution)/shard_map/pallas_call | solution.py:240
  51.9 8.9 shard_map.314
  62.9 3.6 collective-permute-done.3
  69.1 4.4 collective-permute-start.5
  76.6 12.4 %collective-permute-done.5 = bf16[256,512]{1,0:T(8,128)(2,1)S(1)} collective-permute-done((bf16[256,512]{1,0:T(8,128)(2,1)S(1)}, bf16[256,512]{1,0:T(8,128)(2,1)S(1)}, u32[]{:S(2)}, u32[]{:S(2)}) %collective-permute-start.5) | collective-permute-done | bytes 262176 | tf_op jit(solution)/shard_map/ppermute | solution.py:64
  89.0 12.8 %collective-permute-done.6 = bf16[256,512]{1,0:T(8,128)(2,1)S(1)} collective-permute-done((bf16[256,512]{1,0:T(8,128)(2,1)S(1)}, bf16[256,512]{1,0:T(8,128)(2,1)S(1)}, u32[]{:S(2)}, u32[]{:S(2)}) %collective-permute-start.6) | collective-permute-done | bytes 262176 | tf_op jit(solution)/shard_map/ppermute | solution.py:64
  101.8 6.0 collective-permute-done.7
  109.6 12.2 %all-gather.7.cloned.1.call-done = bf16[896,16,256]{2,1,0:T(8,128)(2,1)} async-done(((bf16[28,16,256]{2,1,0:T(8,128)(2,1)}), bf16[896,16,256]{2,1,0:T(8,128)(2,1)}) %all-gather.7.cloned.1.call-update) | async-done | bytes 7340048 | tf_op jit(solution)/shard_map/all_gather | solution.py:1381
  121.7 6.9 shard_map.315
  128.7 9.8 shard_map.316.dense_ref
  147.7 26.1 %shard_map.317 = (bf16[2,4,224,2048]{3,2,1,0:T(8,128)(2,1)}, f32[2,2048]{1,0:T(2,128)}) custom-call(s32[2,32]{1,0:T(2,128)} %pad_add_fusion.place, bf16[2,4,224,2048]{3,2,1,0:T(8,128)(2,1)} %bitcast.241, bf16[8,256,512]{2,1,0:T(8,128)(2,1)} %constant_dynamic-update-slice_fusion.rest_0_, bf16[8,256,512]{2,1,0:T(8,128)(2,1)} %collective-permute-done.4.rest_1_, ...), custom_call_target="tpu_custom_call" | custom-call | flops 15032385536 | bytes 23068672 | tf_op jit(solution)/shard_map/pallas_call | solution.py:240
  205.3 16.1 %shard_map.318 = (bf16[448,2048]{1,0:T(8,128)(2,1)}, f32[2,2048]{1,0:T(2,128)}) custom-call(f32[2]{0:T(128)} %pad_maximum_fusion.16.number, f32[2,2048]{1,0:T(2,128)} %add_add_fusion.12.sums_ref, f32[14,2048]{1,0:T(8,128)} %bitcast.251, f32[448,128]{1,0:T(8,128)} %broadcast_in_dim.39.keep_ref, bf16[2,4,224,2048]{3,2,1,0:T(8,128)(2,1)} %get-tuple-element.324.a_ref, ...), custom_call_target="tpu_custom_call" | custom-call | flops 8455716864 | bytes 26214400 | tf_op jit(solution)/shard_map/pallas_call | solution.py:240
  221.4 8.2 collective-permute-done.26
  237.1 11.9 %collective-permute-start.33 = (f32[2,2048]{1,0:T(2,128)S(1)}, f32[2,2048]{1,0:T(2,128)S(1)}, u32[]{:S(2)}, u32[]{:S(2)}) collective-permute-start(f32[2,2048]{1,0:T(2,128)S(1)} %add_add_fusion.11), channel_id=1, source_target_pairs={{0,16},{1,17},{2,18},{3,19},{4,20},{5,21},{6,22},{7,23},{8,24},{9,... | collective-permute-start | bytes 49160 | tf_op jit(solution)/shard_map/ppermute | solution.py:64
  250.7 3.8 collective-permute-done.34
  258.0 12.5 %shard_map.319 = (bf16[448,2048]{1,0:T(8,128)(2,1)}, bf16[448,2048]{1,0:T(8,128)(2,1)}, f32[2,2048]{1,0:T(2,128)}, f32[8,2048]{1,0:T(8,128)}, f32[8,2048]{1,0:T(...) custom-call(f32[2]{0:T(128)} %pad_maximum_fusion.16.number, s32[2,32]{1,0:T(2,128)} %pad_add_fusion.place, ...), custom_call_target="tpu_custom_call" | custom-call | flops 3758096384 | bytes 15728640 | tf_op jit(solution)/shard_map/pallas_call | solution.py:240
  270.5 11.0 %shard_map.320 = (bf16[2,1,224,2048]{3,2,1,0:T(8,128)(2,1)}, f32[2,2048]{1,0:T(2,128)}) custom-call(s32[2,32]{1,0:T(2,128)} %add_add_fusion.14.place, bf16[2,4,224,2048]{3,2,1,0:T(8,128)(2,1)} %bitcast.242, bf16[16,256,512]{2,1,0:T(8,128)(2,1)} %bitcast.279, bf16[16,256,512]{2,1,0:T(8,128)(2,1)} %collective-permute-done.35.rest_1_), custom_call_target="tpu_custom_call" | custom-call | flops 3758096384 | bytes 12058624 | tf_op jit(solution)/shard_map/pallas_call | solution.py:240
  282.3 17.2 %collective-permute-done.37.rest_1_ = bf16[8,256,512]{2,1,0:T(8,128)(2,1)} collective-permute-done((bf16[8,256,512]{2,1,0:T(8,128)(2,1)S(1)}, bf16[8,256,512]{2,1,0:T(8,128)(2,1)}, u32[]{:S(2)}, u32[]{:S(2)}) %collective-permute-start.37) | collective-permute-done | bytes 2097184 | tf_op jit(solution)/shard_map/ppermute | solution.py:64
  320.0 11.7 %shard_map.321 = (bf16[448,2048]{1,0:T(8,128)(2,1)}, bf16[448,2048]{1,0:T(8,128)(2,1)}, bf16[448,2048]{1,0:T(8,128)(2,1)}, f32[2,2048]{1,0:T(2,128)}) custom-call(f32[2]{0:T(128)} %pad_maximum_fusion.16.number, s32[2,32]{1,0:T(2,128)} %pad_add_fusion.place, f32[2,2048]{1,0:T(2,128)} %get-tuple-element.733.sum2_ref.sums_ref, ...), custom_call_target="tpu_custom_call" | custom-call | flops 3758096384 | bytes 15728640 | tf_op jit(solution)/shard_map/pallas_call | solution.py:240
  331.7 10.0 collective-permute-done.47.refs_1_
  344.6 16.0 %all_to_all.30 = f32[16,2,2048]{2,1,0:T(2,128)S(1)} all-to-all(f32[16,2,2048]{2,1,0:T(2,128)S(1)} %broadcast_in_dim.40), channel_id=1, replica_groups={{0,2,4,6,8,10,12,14,16,18,20,22,24,26,28,30},{1,3,5,7,9,11,13,15,17,19,..., dimensions={0} | all-to-all | bytes 524288 | tf_op jit(solution)/shard_map/all_to_all | solution.py:92
  362.5 6.6 shard_map.322
  369.1 9.9 shard_map.323.dense_ref
  379.5 13.9 %shard_map.324 = (bf16[448,2048]{1,0:T(8,128)(2,1)}, f32[2,2048]{1,0:T(2,128)}) custom-call(f32[2]{0:T(128)} %pad_maximum_fusion.16.number, f32[2,2048]{1,0:T(2,128)} %reduce_sum.146.sums_ref, f32[14,2048]{1,0:T(8,128)} %bitcast.254, f32[448,128]{1,0:T(8,128)} %broadcast_in_dim.39.keep_ref, bf16[2,1,224,2048]{3,2,1,0:T(8,128)(2,1)} %bitcast.287, ...), custom_call_target="tpu_custom_call" | custom-call | flops 8455716864 | bytes 20709376 | tf_op jit(solution)/shard_map/pallas_call | solution.py:240
  409.5 12.8 %shard_map.325 = (bf16[448,2048]{1,0:T(8,128)(2,1)}, bf16[448,2048]{1,0:T(8,128)(2,1)}, f32[2,2048]{1,0:T(2,128)}, f32[8,2048]{1,0:T(8,128)}, f32[8,2048]{1,0:T(...) custom-call(f32[2]{0:T(128)} %pad_maximum_fusion.16.number, s32[2,32]{1,0:T(2,128)} %add_add_fusion.14.place, ...), custom_call_target="tpu_custom_call" | custom-call | flops 3758096384 | bytes 15728640 | tf_op jit(solution)/shard_map/pallas_call | solution.py:240
  438.1 8.8 shard_map.326
  450.1 3.9 all-to-all-start.1
  454.0 8.8 shard_map.327
  465.1 19.6 %shard_map.328 = (bf16[448,2048]{1,0:T(8,128)(2,1)}, bf16[448,2048]{1,0:T(8,128)(2,1)}, f32[2,2048]{1,0:T(2,128)}, f32[8,2048]{1,0:T(8,128)}, f32[8,512]{1,0:T(8,128)}) custom-call(f32[2]{0:T(128)} %pad_maximum_fusion.16.number, s32[2,32]{1,0:T(2,128)} %add_add_fusion.14.place, f32[2,2048]{1,0:T(2,128)} %add_add_fusion.6.sums_ref, ...), custom_call_target="tpu_custom_call" | custom-call | flops 3758096384 | bytes 23068672 | tf_op jit(solution)/shard_map/pallas_call | solution.py:240
  501.7 34.6 %shard_map.329 = (bf16[2,1,224,2048]{3,2,1,0:T(8,128)(2,1)}, f32[2,2048]{1,0:T(2,128)}, bf16[9,64,2048]{2,1,0:T(8,128)(2,1)}) custom-call(f32[2]{0:T(128)} %pad_maximum_fusion.16.number, f32[2,2048]{1,0:T(2,128)} %reduce_sum.146.sums_ref, f32[14,2048]{1,0:T(8,128)} %bitcast.258, f32[448,128]{1,0:T(8,128)} %broadcast_in_dim.39.keep_ref, ...), custom_call_target="tpu_custom_call" | custom-call | flops 25367150592 | bytes 20709376 | tf_op jit(solution)/shard_map/pallas_call | solution.py:240
  539.4 4.5 all-to-all-start.2
  544.6 11.2 %shard_map.330 = bf16[16,256,512]{2,1,0:T(8,128)(2,1)} custom-call(s32[2,16]{1,0:T(2,128)} %pad_add_fusion.2.order, bf16[448,2048]{1,0:T(8,128)(2,1)} %get-tuple-element.417.refs_0_, bf16[448,2048]{1,0:T(8,128)(2,1)} %get-tuple-element.418.refs_1_, bf16[448,2048]{1,0:T(8,128)(2,1)} %copy-done.95, bf16[448,2048]{1,0:T(8,128)(2,1)} %copy-done.96), custom_call_target="tpu_custom_call" | custom-call | flops 3758096384 | bytes 11534336 | tf_op jit(solution)/shard_map/pallas_call | solution.py:240
  561.6 17.4 %shard_map.331 = (bf16[448,2048]{1,0:T(8,128)(2,1)}, bf16[448,2048]{1,0:T(8,128)(2,1)}, f32[3,2048]{1,0:T(4,128)}) custom-call(f32[2]{0:T(128)} %pad_maximum_fusion.16.number, s32[2,32]{1,0:T(2,128)} %pad_add_fusion.place, f32[2,2048]{1,0:T(2,128)} %reduce_sum.146.sums_ref, f32[2,2048]{1,0:T(2,128)} %reduce_sum.148.back_ref, ...), custom_call_target="tpu_custom_call" | custom-call | flops 3758096384 | bytes 26738688 | tf_op jit(solution)/shard_map/pallas_call | solution.py:240
  578.9 6.9 collective-permute-done.80
  608.5 19.8 %shard_map.333 = (bf16[448,2048]{1,0:T(8,128)(2,1)}, bf16[448,2048]{1,0:T(8,128)(2,1)}, f32[2,2048]{1,0:T(2,128)}, f32[8,2048]{1,0:T(8,128)}, f32[8,512]{1,0:T(8,128)}) custom-call(f32[2]{0:T(128)} %pad_maximum_fusion.16.number, s32[2,32]{1,0:T(2,128)} %pad_add_fusion.place, f32[2,2048]{1,0:T(2,128)} %get-tuple-element.733.sum2_ref.sums_ref, ...), custom_call_target="tpu_custom_call" | custom-call | flops 3758096384 | bytes 23068672 | tf_op jit(solution)/shard_map/pallas_call | solution.py:240
  640.7 4.3 all-to-all-start.3
  647.1 11.3 %shard_map.334 = bf16[16,256,512]{2,1,0:T(8,128)(2,1)} custom-call(s32[2,16]{1,0:T(2,128)} %pad_add_fusion.2.order, bf16[448,2048]{1,0:T(8,128)(2,1)} %get-tuple-element.447.refs_0_, bf16[448,2048]{1,0:T(8,128)(2,1)} %get-tuple-element.448.refs_1_, bf16[448,2048]{1,0:T(8,128)(2,1)} %collective-permute-done.52.refs_2_, ...), custom_call_target="tpu_custom_call" | custom-call | flops 3758096384 | bytes 11534336 | tf_op jit(solution)/shard_map/pallas_call | solution.py:240
  662.1 11.2 %shard_map.335 = bf16[16,256,512]{2,1,0:T(8,128)(2,1)} custom-call(s32[2,16]{1,0:T(2,128)} %pad_add_fusion.2.order, bf16[448,2048]{1,0:T(8,128)(2,1)} %get-tuple-element.364.refs_0_, bf16[448,2048]{1,0:T(8,128)(2,1)} %get-tuple-element.451.refs_1_, bf16[448,2048]{1,0:T(8,128)(2,1)} %copy-done.93, bf16[448,2048]{1,0:T(8,128)(2,1)} %collective-permute-done.92.refs_3_), custom_call_target="tpu_custom_call" | custom-call | flops 3758096384 | bytes 11534336 | tf_op jit(solution)/shard_map/pallas_call | solution.py:240
  680.8 4.9 all-to-all-start.4
  693.5 41.3 %shard_map.336 = (bf16[2,4,224,2048]{3,2,1,0:T(8,128)(2,1)}, f32[2,2048]{1,0:T(2,128)}, bf16[9,64,2048]{2,1,0:T(8,128)(2,1)}) custom-call(f32[2]{0:T(128)} %pad_maximum_fusion.16.number, f32[2,2048]{1,0:T(2,128)} %add_add_fusion.12.sums_ref, f32[14,2048]{1,0:T(8,128)} %bitcast.261, f32[448,128]{1,0:T(8,128)} %broadcast_in_dim.39.keep_ref, ...), custom_call_target="tpu_custom_call" | custom-call | flops 25367150592 | bytes 26214400 | tf_op jit(solution)/shard_map/pallas_call | solution.py:240
  736.3 12.0 %collective-permute-done.98 = bf16[8,256,512]{2,1,0:T(8,128)(2,1)} collective-permute-done((bf16[8,256,512]{2,1,0:T(8,128)(2,1)}, bf16[8,256,512]{2,1,0:T(8,128)(2,1)}, u32[]{:S(2)}, u32[]{:S(2)}) %collective-permute-start.98) | collective-permute-done | bytes 2097184 | tf_op jit(solution)/shard_map/ppermute | solution.py:64
  748.5 4.3 add_convert_fusion.5
  752.8 3.5 add_convert_fusion.4
  757.1 5.7 all-to-all-start.5
  767.2 11.7 %shard_map.337 = (bf16[448,2048]{1,0:T(8,128)(2,1)}, bf16[448,2048]{1,0:T(8,128)(2,1)}) custom-call(f32[2]{0:T(128)} %pad_maximum_fusion.16.number, s32[2,32]{1,0:T(2,128)} %add_add_fusion.14.place, f32[2,2048]{1,0:T(2,128)} %get-tuple-element.732.sum3_ref.sums_ref, f32[2,2048]{1,0:T(2,128)} %pad_maximum_fusion.15.back_ref, f32[14,2048]{1,0:T(8,128)} %bitcast.262, ...), custom_call_target="tpu_custom_call" | custom-call | flops 3758096384 | bytes 19398656 | tf_op jit(solution)/shard_map/pallas_call | solution.py:240
  783.2 15.1 %shard_map.339 = (bf16[2,4,224,2048]{3,2,1,0:T(8,128)(2,1)}, bf16[4,2048,512]{2,1,0:T(8,128)(2,1)}) custom-call(f32[2]{0:T(128)} %pad_maximum_fusion.16.number, f32[2,2048]{1,0:T(2,128)} %add_add_fusion.12.sums_ref, f32[2,2048]{1,0:T(2,128)} %reduce_sum.151.back_ref, f32[14,2048]{1,0:T(8,128)} %bitcast.263, f32[448,128]{1,0:T(8,128)} %broadcast_in_dim.39.keep_ref, ...), custom_call_target="tpu_custom_call" | custom-call | bytes 29360128 | tf_op jit(solution)/shard_map/pallas_call | solution.py:240
  822.5 11.2 %shard_map.340 = bf16[16,256,512]{2,1,0:T(8,128)(2,1)} custom-call(s32[2,16]{1,0:T(2,128)} %pad_add_fusion.2.order, bf16[2,4,224,2048]{3,2,1,0:T(8,128)(2,1)} %bitcast.244, bf16[2,4,224,2048]{3,2,1,0:T(8,128)(2,1)} %collective-permute-done.70.x1_ref, bf16[448,2048]{1,0:T(8,128)(2,1)} %get-tuple-element.493.g0_ref, ...), custom_call_target="tpu_custom_call" | custom-call | flops 3758096384 | bytes 11534336 | tf_op jit(solution)/shard_map/pallas_call | solution.py:240
  844.0 16.2 %shard_map.341 = bf16[2,2,224,2048]{3,2,1,0:T(8,128)(2,1)} custom-call(s32[2,32]{1,0:T(2,128)} %pad_add_fusion.place, bf16[2,4,224,2048]{3,2,1,0:T(8,128)(2,1)} %get-tuple-element.515.da_ref, bf16[448,2048]{1,0:T(8,128)(2,1)} %get-tuple-element.516.side_ref, bf16[8,256,512]{2,1,0:T(8,128)(2,1)} %constant_dynamic-update-slice_fusion.rest_0_, ...), custom_call_target="tpu_custom_call" | custom-call | flops 7516192768 | bytes 15728640 | tf_op jit(solution)/shard_map/pallas_call | solution.py:240
  866.7 16.4 %shard_map.342 = bf16[8,256,512]{2,1,0:T(8,128)(2,1)} custom-call(s32[2,8]{1,0:T(2,128)} %slice.548.spots, bf16[2,4,224,2048]{3,2,1,0:T(8,128)(2,1)} %bitcast.245, bf16[2,4,224,2048]{3,2,1,0:T(8,128)(2,1)} %collective-permute-done.70.x1_ref, bf16[4,2048,512]{2,1,0:T(8,128)(2,1)} %get-tuple-element.506.g0_ref, ...), custom_call_target="tpu_custom_call" | custom-call | flops 7516192768 | bytes 14680064 | tf_op jit(solution)/shard_map/pallas_call | solution.py:400
  889.4 4.2 add_convert_fusion
  895.1 16.1 %shard_map.343 = bf16[8,256,512]{2,1,0:T(8,128)(2,1)} custom-call(s32[2,8]{1,0:T(2,128)} %bitcast.316, bf16[2,4,224,2048]{3,2,1,0:T(8,128)(2,1)} %bitcast.246, bf16[2,4,224,2048]{3,2,1,0:T(8,128)(2,1)} %collective-permute-done.70.x1_ref, bf16[4,2048,512]{2,1,0:T(8,128)(2,1)} %get-tuple-element.506.g0_ref, bf16[4,2048,512]{2,1,0:T(8,128)(2,1)} %collective-permute-done.106.g1_ref), custom_call_target="tpu_custom_call" | custom-call | flops 7516192768 | bytes 14680064 | tf_op jit(solution)/shard_map/pallas_call | solution.py:400
  911.2 16.4 %shard_map.344 = bf16[2,2,224,2048]{3,2,1,0:T(8,128)(2,1)} custom-call(s32[2,32]{1,0:T(2,128)} %pad_add_fusion.place, bf16[2,4,224,2048]{3,2,1,0:T(8,128)(2,1)} %get-tuple-element.515.da_ref, bf16[448,2048]{1,0:T(8,128)(2,1)} %get-tuple-element.516.side_ref, bf16[8,256,512]{2,1,0:T(8,128)(2,1)} %constant_dynamic-update-slice_fusion.rest_0_, ...), custom_call_target="tpu_custom_call" | custom-call | flops 7516192768 | bytes 15728640 | tf_op jit(solution)/shard_map/pallas_call | solution.py:240
  927.7 3.5 add_convert_fusion.2
  942.8 12.6 %shard_map.345 = bf16[2,28,28,2016]{3,2,1,0:T(8,128)(2,1)} custom-call(bf16[128,128]{1,0:T(8,128)(2,1)} %constant.148.clone.select, bf16[2,2,14,16,2048]{4,3,2,1,0:T(8,128)(2,1)} %bitcast.281, bf16[2,2,14,16,2048]{4,3,2,1,0:T(8,128)(2,1)} %bitcast.282), custom_call_target="tpu_custom_call" | custom-call | bytes 14680064 | tf_op jit(solution)/shard_map/pallas_call | solution.py:240
  956.7 4.5 collective-permute-done.119
  961.2 4.7 collective-permute-start.121
  968.6 13.2 %copy.148 = bf16[2,28,28,2016]{3,0,2,1:T(2,128)(2,1)} copy(bf16[2,28,28,2016]{3,2,1,0:T(8,128)(2,1)} %shard_map.345) | data formatting | bytes 12644352
  991.4 4.1 collective-permute-start.128
  1001.9 12.6 %collective-permute-done.128 = bf16[256,512]{1,0:T(8,128)(2,1)S(1)} collective-permute-done((bf16[256,512]{1,0:T(8,128)(2,1)S(1)}, bf16[256,512]{1,0:T(8,128)(2,1)S(1)}, u32[]{:S(2)}, u32[]{:S(2)}) %collective-permute-start.128) | collective-permute-done | bytes 262176 | tf_op jit(solution)/shard_map/ppermute | solution.py:64
  1020.1 3.5 copy.156
  1056.3 5.6 collective-permute-start.138
  1063.4 3.8 collective-permute-done.139
  1074.4 5.6 fusion.78
  (673 shorter events, 372.2 us)
Async XLA Ops:
  7.2 114.5 %all-gather.7.cloned.1.call-start = ((), (), s32[]{:S(2)}) async-start(), calls=%async_computation.6 | async-start | bytes 7569408 | tf_op jit(solution)/shard_map/all_gather | solution.py:1381
  13.1 242.0 %all-gather.9.cloned.1.call-start = ((), (), s32[]{:S(2)}) async-start(), calls=%async_computation.7 | async-start | bytes 4456448 | tf_op jit(solution)/shard_map/all_gather | solution.py:86
  19.0 29.0 %collective-permute-start = (bf16[256,512]{1,0:T(8,128)(2,1)S(1)}, bf16[256,512]{1,0:T(8,128)(2,1)S(1)}, u32[]{:S(2)}, u32[]{:S(2)}) collective-permute-start(bf16[256,512]{1,0:T(8,128)(2,1)S(1)} %get-tuple-element.703), channel_id=1, source_target_pairs={{0,8},{1,9},{2,10},{3,11},{4,12},{5,13},{6,14},{7,15},{8,0},{9,1},... | collective-permute-start | bytes 786440 | tf_op jit(solution)/shard_map/ppermute | solution.py:64
  22.0 26.2 %collective-permute-start.1 = (bf16[256,512]{1,0:T(8,128)(2,1)S(1)}, bf16[256,512]{1,0:T(8,128)(2,1)S(1)}, u32[]{:S(2)}, u32[]{:S(2)}) collective-permute-start(bf16[256,512]{1,0:T(8,128)(2,1)S(1)} %get-tuple-element.703), channel_id=1, source_target_pairs={{0,16},{1,17},{2,18},{3,19},{4,20},{5,21},{6,22},{7,23},{8,24},{9,... | collective-permute-start | bytes 786440 | tf_op jit(solution)/shard_map/ppermute | solution.py:64
  24.6 23.7 %collective-permute-start.2 = (bf16[256,512]{1,0:T(8,128)(2,1)S(1)}, bf16[256,512]{1,0:T(8,128)(2,1)S(1)}, u32[]{:S(2)}, u32[]{:S(2)}) collective-permute-start(bf16[256,512]{1,0:T(8,128)(2,1)S(1)} %get-tuple-element.703), channel_id=1, source_target_pairs={{0,24},{1,25},{2,26},{3,27},{4,28},{5,29},{6,30},{7,31},{8,16},{9,... | collective-permute-start | bytes 786440 | tf_op jit(solution)/shard_map/ppermute | solution.py:64
  48.4 18.2 %collective-permute-start.3 = (bf16[4,256,512]{2,1,0:T(8,128)(2,1)S(1)}, bf16[4,256,512]{2,1,0:T(8,128)(2,1)S(1)}, u32[]{:S(2)}, u32[]{:S(2)}) collective-permute-start(bf16[4,256,512]{2,1,0:T(8,128)(2,1)S(1)} %pad_maximum_fusion.2), channel_id=1, source_target_pairs={{0,4},{1,3},{2,6},{3,1},{4,0},{5,7},{6,2},{7,5},{8,12},{9,11},{10,... | collective-permute-start | bytes 3145736 | tf_op jit(solution)/shard_map/ppermute | solution.py:64
  67.6 40.2 %collective-permute-start.4 = (bf16[8,256,512]{2,1,0:T(8,128)(2,1)}, bf16[8,256,512]{2,1,0:T(8,128)(2,1)}, u32[]{:S(2)}, u32[]{:S(2)}) collective-permute-start(bf16[8,256,512]{2,1,0:T(8,128)(2,1)} %constant_dynamic-update-slice_fusion.rest_0_), channel_id=1, source_target_pairs={{0,2},{1,5},{2,0},{3,7},{4,6},{5,1},{6,4},{7,3},{8,10},{9,13},{10,... | collective-permute-start | bytes 6291464 | tf_op jit(solution)/shard_map/ppermute | solution.py:64
  69.1 20.0 %collective-permute-start.5 = (bf16[256,512]{1,0:T(8,128)(2,1)S(1)}, bf16[256,512]{1,0:T(8,128)(2,1)S(1)}, u32[]{:S(2)}, u32[]{:S(2)}) collective-permute-start(bf16[256,512]{1,0:T(8,128)(2,1)S(1)} %get-tuple-element.298), channel_id=1, source_target_pairs={{0,8},{1,9},{2,10},{3,11},{4,12},{5,13},{6,14},{7,15},{8,0},{9,1},... | collective-permute-start | bytes 786440 | tf_op jit(solution)/shard_map/ppermute | solution.py:64
  73.4 28.4 %collective-permute-start.6 = (bf16[256,512]{1,0:T(8,128)(2,1)S(1)}, bf16[256,512]{1,0:T(8,128)(2,1)S(1)}, u32[]{:S(2)}, u32[]{:S(2)}) collective-permute-start(bf16[256,512]{1,0:T(8,128)(2,1)S(1)} %get-tuple-element.298), channel_id=1, source_target_pairs={{0,16},{1,17},{2,18},{3,19},{4,20},{5,21},{6,22},{7,23},{8,24},{9,... | collective-permute-start | bytes 786440 | tf_op jit(solution)/shard_map/ppermute | solution.py:64
  74.3 33.4 %collective-permute-start.7 = (bf16[256,512]{1,0:T(8,128)(2,1)S(1)}, bf16[256,512]{1,0:T(8,128)(2,1)S(1)}, u32[]{:S(2)}, u32[]{:S(2)}) collective-permute-start(bf16[256,512]{1,0:T(8,128)(2,1)S(1)} %get-tuple-element.298), channel_id=1, source_target_pairs={{0,24},{1,25},{2,26},{3,27},{4,28},{5,29},{6,30},{7,31},{8,16},{9,... | collective-permute-start | bytes 786440 | tf_op jit(solution)/shard_map/ppermute | solution.py:64
  75.8 62.6 %collective-permute-start.8 = (bf16[8,256,512]{2,1,0:T(8,128)(2,1)}, bf16[8,256,512]{2,1,0:T(8,128)(2,1)}, u32[]{:S(2)}, u32[]{:S(2)}) collective-permute-start(bf16[8,256,512]{2,1,0:T(8,128)(2,1)} %constant_dynamic-update-slice_fusion.rest_0_), channel_id=1, source_target_pairs={{0,1},{1,0},{2,3},{3,2},{4,5},{5,4},{6,7},{7,6},{8,9},{9,8},{10,11... | collective-permute-start | bytes 6291464 | tf_op jit(solution)/shard_map/ppermute | solution.py:64
  107.8 30.7 %collective-permute-start.9 = (bf16[8,256,512]{2,1,0:T(8,128)(2,1)}, bf16[8,256,512]{2,1,0:T(8,128)(2,1)}, u32[]{:S(2)}, u32[]{:S(2)}) collective-permute-start(bf16[8,256,512]{2,1,0:T(8,128)(2,1)} %collective-permute-done.4.rest_1_), channel_id=1, source_target_pairs={{0,1},{1,0},{2,3},{3,2},{4,5},{5,4},{6,7},{7,6},{8,9},{9,8},{10,11... | collective-permute-start | bytes 6291464 | tf_op jit(solution)/shard_map/ppermute | solution.py:64
  108.7 29.7 %collective-permute-start.10 = (bf16[4,256,512]{2,1,0:T(8,128)(2,1)S(1)}, bf16[4,256,512]{2,1,0:T(8,128)(2,1)S(1)}, u32[]{:S(2)}, u32[]{:S(2)}) collective-permute-start(bf16[4,256,512]{2,1,0:T(8,128)(2,1)S(1)} %pad_maximum_fusion.3), channel_id=1, source_target_pairs={{0,4},{1,3},{2,6},{3,1},{4,0},{5,7},{6,2},{7,5},{8,12},{9,11},{10,... | collective-permute-start | bytes 3145736 | tf_op jit(solution)/shard_map/ppermute | solution.py:64
  138.5 240.5 %all-gather.11.cloned.1.call-start = ((), (), s32[]{:S(2)}) async-start(), calls=%async_computation.8 | async-start | bytes 4456448 | tf_op jit(solution)/shard_map/all_gather | solution.py:86
  141.6 32.3 %collective-permute-start.11 = (bf16[8,256,512]{2,1,0:T(8,128)(2,1)S(1)}, bf16[8,256,512]{2,1,0:T(8,128)(2,1)}, u32[]{:S(2)}, u32[]{:S(2)}) collective-permute-start(bf16[8,256,512]{2,1,0:T(8,128)(2,1)S(1)} %constant_dynamic-update-slice_fusion.5.rest_0_), channel_id=1, source_target_pairs={{0,2},{1,5},{2,0},{3,7},{4,6},{5,1},{6,4},{7,3},{8,10},{9,13},{10,... | collective-permute-start | bytes 6291464 | tf_op jit(solution)/shard_map/ppermute | solution.py:64
  143.3 30.5 %collective-permute-start.12 = (bf16[256,512]{1,0:T(8,128)(2,1)}, bf16[256,512]{1,0:T(8,128)(2,1)S(1)}, u32[]{:S(2)}, u32[]{:S(2)}) collective-permute-start(bf16[256,512]{1,0:T(8,128)(2,1)} %get-tuple-element.312), channel_id=1, source_target_pairs={{0,8},{1,9},{2,10},{3,11},{4,12},{5,13},{6,14},{7,15},{8,0},{9,1},... | collective-permute-start | bytes 786440 | tf_op jit(solution)/shard_map/ppermute | solution.py:64
  143.3 30.5 %collective-permute-start.13 = (bf16[256,512]{1,0:T(8,128)(2,1)}, bf16[256,512]{1,0:T(8,128)(2,1)S(1)}, u32[]{:S(2)}, u32[]{:S(2)}) collective-permute-start(bf16[256,512]{1,0:T(8,128)(2,1)} %get-tuple-element.312), channel_id=1, source_target_pairs={{0,16},{1,17},{2,18},{3,19},{4,20},{5,21},{6,22},{7,23},{8,24},{9,... | collective-permute-start | bytes 786440 | tf_op jit(solution)/shard_map/ppermute | solution.py:64
  145.9 27.9 %collective-permute-start.14 = (bf16[256,512]{1,0:T(8,128)(2,1)}, bf16[256,512]{1,0:T(8,128)(2,1)S(1)}, u32[]{:S(2)}, u32[]{:S(2)}) collective-permute-start(bf16[256,512]{1,0:T(8,128)(2,1)} %get-tuple-element.312), channel_id=1, source_target_pairs={{0,24},{1,25},{2,26},{3,27},{4,28},{5,29},{6,30},{7,31},{8,16},{9,... | collective-permute-start | bytes 786440 | tf_op jit(solution)/shard_map/ppermute | solution.py:64
  195.6 34.0 %collective-permute-start.24 = (bf16[4,256,512]{2,1,0:T(8,128)(2,1)S(1)}, bf16[4,256,512]{2,1,0:T(8,128)(2,1)S(1)}, u32[]{:S(2)}, u32[]{:S(2)}) collective-permute-start(bf16[4,256,512]{2,1,0:T(8,128)(2,1)S(1)} %pad_maximum_fusion.4), channel_id=1, source_target_pairs={{0,4},{1,3},{2,6},{3,1},{4,0},{5,7},{6,2},{7,5},{8,12},{9,11},{10,... | collective-permute-start | bytes 3145736 | tf_op jit(solution)/shard_map/ppermute | solution.py:64
  200.1 21.4 %collective-permute-start.25 = (bf16[25,16,256]{2,1,0:T(8,128)(2,1)S(1)}, bf16[25,16,256]{2,1,0:T(8,128)(2,1)S(1)}, u32[]{:S(2)}, u32[]{:S(2)}) collective-permute-start(bf16[25,16,256]{2,1,0:T(8,128)(2,1)S(1)} %bitcast.302), channel_id=1, source_target_pairs={{0,8},{1,9},{2,10},{3,11},{4,12},{5,13},{6,14},{7,15},{8,0},{9,1},... | collective-permute-start | bytes 614408 | tf_op jit(solution)/shard_map/ppermute | solution.py:64
  200.1 29.6 %collective-permute-start.26 = (bf16[25,16,256]{2,1,0:T(8,128)(2,1)S(1)}, bf16[25,16,256]{2,1,0:T(8,128)(2,1)S(1)}, u32[]{:S(2)}, u32[]{:S(2)}) collective-permute-start(bf16[25,16,256]{2,1,0:T(8,128)(2,1)S(1)} %bitcast.303), channel_id=1, source_target_pairs={{0,16},{1,17},{2,18},{3,19},{4,20},{5,21},{6,22},{7,23},{8,24},{9,... | collective-permute-start | bytes 614408 | tf_op jit(solution)/shard_map/ppermute | solution.py:64
  202.7 27.0 %collective-permute-start.27 = (bf16[25,16,256]{2,1,0:T(8,128)(2,1)S(1)}, bf16[25,16,256]{2,1,0:T(8,128)(2,1)S(1)}, u32[]{:S(2)}, u32[]{:S(2)}) collective-permute-start(bf16[25,16,256]{2,1,0:T(8,128)(2,1)S(1)} %bitcast.304), channel_id=1, source_target_pairs={{0,24},{1,25},{2,26},{3,27},{4,28},{5,29},{6,30},{7,31},{8,16},{9,... | collective-permute-start | bytes 614408 | tf_op jit(solution)/shard_map/ppermute | solution.py:64
  255.2 44.3 %collective-permute-start.37 = (bf16[8,256,512]{2,1,0:T(8,128)(2,1)S(1)}, bf16[8,256,512]{2,1,0:T(8,128)(2,1)}, u32[]{:S(2)}, u32[]{:S(2)}) collective-permute-start(bf16[8,256,512]{2,1,0:T(8,128)(2,1)S(1)} %pad_maximum_fusion.rest_0_), channel_id=1, source_target_pairs={{0,2},{1,5},{2,0},{3,7},{4,6},{5,1},{6,4},{7,3},{8,10},{9,13},{10,... | collective-permute-start | bytes 6291464 | tf_op jit(solution)/shard_map/ppermute | solution.py:64
  257.1 25.2 %collective-permute-start.36 = (bf16[4,25,16,256]{3,2,1,0:T(8,128)(2,1)S(1)}, bf16[4,25,16,256]{3,2,1,0:T(8,128)(2,1)}, u32[]{:S(2)}, u32[]{:S(2)}) collective-permute-start(bf16[4,25,16,256]{3,2,1,0:T(8,128)(2,1)S(1)} %pad_maximum_fusion.6), channel_id=1, source_target_pairs={{0,4},{1,3},{2,6},{3,1},{4,0},{5,7},{6,2},{7,5},{8,12},{9,11},{10,... | collective-permute-start | bytes 2457608 | tf_op jit(solution)/shard_map/ppermute | solution.py:64
  319.2 22.5 %collective-permute-start.48 = (bf16[448,2048]{1,0:T(8,128)(2,1)}, bf16[448,2048]{1,0:T(8,128)(2,1)S(1)}, u32[]{:S(2)}, u32[]{:S(2)}) collective-permute-start(bf16[448,2048]{1,0:T(8,128)(2,1)} %get-tuple-element.364.refs_0_), channel_id=1, source_target_pairs={{0,1},{1,0},{2,3},{3,2},{4,5},{5,4},{6,7},{7,6},{8,9},{9,8},{10,11... | collective-permute-start | bytes 5505032 | tf_op jit(solution)/shard_map/ppermute | solution.py:64
  319.2 22.5 %collective-permute-start.47 = (bf16[8,25,16,256]{3,2,1,0:T(8,128)(2,1)}, bf16[8,25,16,256]{3,2,1,0:T(8,128)(2,1)S(1)}, u32[]{:S(2)}, u32[]{:S(2)}) collective-permute-start(bf16[8,25,16,256]{3,2,1,0:T(8,128)(2,1)} %pad_maximum_fusion.1.refs_0_), channel_id=1, source_target_pairs={{0,2},{1,5},{2,0},{3,7},{4,6},{5,1},{6,4},{7,3},{8,10},{9,13},{10,... | collective-permute-start | bytes 4915208 | tf_op jit(solution)/shard_map/ppermute | solution.py:64
  465.1 19.6 %collective-permute-start.70 = (bf16[2,4,224,2048]{3,2,1,0:T(8,128)(2,1)}, bf16[2,4,224,2048]{3,2,1,0:T(8,128)(2,1)}, u32[]{:S(2)}, u32[]{:S(2)}) collective-permute-start(bf16[2,4,224,2048]{3,2,1,0:T(8,128)(2,1)} %bitcast.243), channel_id=1, source_target_pairs={{0,1},{1,0},{2,3},{3,2},{4,5},{5,4},{6,7},{7,6},{8,9},{9,8},{10,11... | collective-permute-start | bytes 22020104 | tf_op jit(solution)/shard_map/ppermute | solution.py:64
  559.6 26.2 %collective-permute-start.80 = (bf16[8,256,512]{2,1,0:T(8,128)(2,1)}, bf16[8,256,512]{2,1,0:T(8,128)(2,1)S(1)}, u32[]{:S(2)}, u32[]{:S(2)}) collective-permute-start(bf16[8,256,512]{2,1,0:T(8,128)(2,1)} %slice.489), channel_id=1, source_target_pairs={{0,2},{1,5},{2,0},{3,7},{4,6},{5,1},{6,4},{7,3},{8,10},{9,13},{10,... | collective-permute-start | bytes 6291464 | tf_op jit(solution)/shard_map/ppermute | solution.py:64
  588.0 18.3 %collective-permute-start.88 = (bf16[448,2048]{1,0:T(8,128)(2,1)}, bf16[448,2048]{1,0:T(8,128)(2,1)}, u32[]{:S(2)}, u32[]{:S(2)}) collective-permute-start(bf16[448,2048]{1,0:T(8,128)(2,1)} %get-tuple-element.448.refs_1_), channel_id=1, source_target_pairs={{0,1},{1,0},{2,3},{3,2},{4,5},{5,4},{6,7},{7,6},{8,9},{9,8},{10,11... | collective-permute-start | bytes 5505032 | tf_op jit(solution)/shard_map/ppermute | solution.py:64
  606.3 22.0 %collective-permute-start.90 = (bf16[16,9,16,256]{3,2,1,0:T(8,128)(2,1)}, bf16[16,9,16,256]{3,2,1,0:T(8,128)(2,1)}, u32[]{:S(2)}, u32[]{:S(2)}) collective-permute-start(bf16[16,9,16,256]{3,2,1,0:T(8,128)(2,1)} %slice.632), channel_id=1, source_target_pairs={{0,1},{1,0},{2,3},{3,2},{4,5},{5,4},{6,7},{7,6},{8,9},{9,8},{10,11... | collective-permute-start | bytes 3538952 | tf_op jit(solution)/shard_map/ppermute | solution.py:64
  606.3 21.9 %collective-permute-start.89 = (bf16[4,256,512]{2,1,0:T(8,128)(2,1)}, bf16[4,256,512]{2,1,0:T(8,128)(2,1)}, u32[]{:S(2)}, u32[]{:S(2)}) collective-permute-start(bf16[4,256,512]{2,1,0:T(8,128)(2,1)} %get-tuple-element.440), channel_id=1, source_target_pairs={{0,4},{1,3},{2,6},{3,1},{4,0},{5,7},{6,2},{7,5},{8,12},{9,11},{10,... | collective-permute-start | bytes 3145736 | tf_op jit(solution)/shard_map/ppermute | solution.py:64
  630.4 28.6 %collective-permute-start.92 = (bf16[448,2048]{1,0:T(8,128)(2,1)}, bf16[448,2048]{1,0:T(8,128)(2,1)}, u32[]{:S(2)}, u32[]{:S(2)}) collective-permute-start(bf16[448,2048]{1,0:T(8,128)(2,1)} %get-tuple-element.451.refs_1_), channel_id=1, source_target_pairs={{0,1},{1,0},{2,3},{3,2},{4,5},{5,4},{6,7},{7,6},{8,9},{9,8},{10,11... | collective-permute-start | bytes 5505032 | tf_op jit(solution)/shard_map/ppermute | solution.py:64
  680.8 54.1 %all-to-all-start.4 = ((f32[32,2,3072]{2,1,0:T(2,128)}), f32[32,2,3072]{2,1,0:T(2,128)S(1)}, u32[]{:S(2)}, u32[]{:S(2)}) async-start(f32[32,2,3072]{2,1,0:T(2,128)} %pad_maximum_fusion.7), calls=%async_computation.4 | async-start | bytes 1572864 | tf_op jit(solution)/shard_map/all_to_all | solution.py:96
  685.7 50.6 %collective-permute-start.93 = (bf16[8,256,512]{2,1,0:T(8,128)(2,1)}, bf16[8,256,512]{2,1,0:T(8,128)(2,1)}, u32[]{:S(2)}, u32[]{:S(2)}) collective-permute-start(bf16[8,256,512]{2,1,0:T(8,128)(2,1)} %slice.494), channel_id=1, source_target_pairs={{0,2},{1,5},{2,0},{3,7},{4,6},{5,1},{6,4},{7,3},{8,10},{9,13},{10,... | collective-permute-start | bytes 6291464 | tf_op jit(solution)/shard_map/ppermute | solution.py:64
  687.7 48.6 %collective-permute-start.94 = (bf16[8,9,16,256]{3,2,1,0:T(8,128)(2,1)S(1)}, bf16[8,9,16,256]{3,2,1,0:T(8,128)(2,1)S(1)}, u32[]{:S(2)}, u32[]{:S(2)}) collective-permute-start(bf16[8,9,16,256]{3,2,1,0:T(8,128)(2,1)S(1)} %copy-done.46), channel_id=1, source_target_pairs={{0,2},{1,5},{2,0},{3,7},{4,6},{5,1},{6,4},{7,3},{8,10},{9,13},{10,... | collective-permute-start | bytes 1769480 | tf_op jit(solution)/shard_map/ppermute | solution.py:64
  687.8 48.5 %collective-permute-start.96 = (bf16[256,512]{1,0:T(8,128)(2,1)}, bf16[256,512]{1,0:T(8,128)(2,1)S(1)}, u32[]{:S(2)}, u32[]{:S(2)}) collective-permute-start(bf16[256,512]{1,0:T(8,128)(2,1)} %get-tuple-element.473), channel_id=1, source_target_pairs={{0,16},{1,17},{2,18},{3,19},{4,20},{5,21},{6,22},{7,23},{8,24},{9,... | collective-permute-start | bytes 786440 | tf_op jit(solution)/shard_map/ppermute | solution.py:64
  690.6 45.7 %collective-permute-start.97 = (bf16[256,512]{1,0:T(8,128)(2,1)}, bf16[256,512]{1,0:T(8,128)(2,1)S(1)}, u32[]{:S(2)}, u32[]{:S(2)}) collective-permute-start(bf16[256,512]{1,0:T(8,128)(2,1)} %get-tuple-element.474), channel_id=1, source_target_pairs={{0,24},{1,25},{2,26},{3,27},{4,28},{5,29},{6,30},{7,31},{8,16},{9,... | collective-permute-start | bytes 786440 | tf_op jit(solution)/shard_map/ppermute | solution.py:64
  692.1 56.3 %collective-permute-start.98 = (bf16[8,256,512]{2,1,0:T(8,128)(2,1)}, bf16[8,256,512]{2,1,0:T(8,128)(2,1)}, u32[]{:S(2)}, u32[]{:S(2)}) collective-permute-start(bf16[8,256,512]{2,1,0:T(8,128)(2,1)} %slice.637), channel_id=1, source_target_pairs={{0,2},{1,5},{2,0},{3,7},{4,6},{5,1},{6,4},{7,3},{8,10},{9,13},{10,... | collective-permute-start | bytes 6291464 | tf_op jit(solution)/shard_map/ppermute | solution.py:64
  757.1 21.7 %all-to-all-start.5 = ((f32[16,2,2048]{2,1,0:T(2,128)}), f32[16,2,2048]{2,1,0:T(2,128)S(1)}, u32[]{:S(2)}, u32[]{:S(2)}) async-start(f32[16,2,2048]{2,1,0:T(2,128)} %broadcast_in_dim.90), calls=%async_computation.5 | async-start | bytes 524288 | tf_op jit(solution)/shard_map/all_to_all | solution.py:92
  780.6 18.8 %collective-permute-start.100 = (bf16[448,2048]{1,0:T(8,128)(2,1)}, bf16[448,2048]{1,0:T(8,128)(2,1)}, u32[]{:S(2)}, u32[]{:S(2)}) collective-permute-start(bf16[448,2048]{1,0:T(8,128)(2,1)} %get-tuple-element.493.g0_ref), channel_id=1, source_target_pairs={{0,1},{1,0},{2,3},{3,2},{4,5},{5,4},{6,7},{7,6},{8,9},{9,8},{10,11... | collective-permute-start | bytes 5505032 | tf_op jit(solution)/shard_map/ppermute | solution.py:64
  781.0 18.4 %collective-permute-start.103 = (bf16[16,9,16,256]{3,2,1,0:T(8,128)(2,1)}, bf16[16,9,16,256]{3,2,1,0:T(8,128)(2,1)}, u32[]{:S(2)}, u32[]{:S(2)}) collective-permute-start(bf16[16,9,16,256]{3,2,1,0:T(8,128)(2,1)} %slice.524), channel_id=1, source_target_pairs={{0,1},{1,0},{2,3},{3,2},{4,5},{5,4},{6,7},{7,6},{8,9},{9,8},{10,11... | collective-permute-start | bytes 3538952 | tf_op jit(solution)/shard_map/ppermute | solution.py:64
  781.1 18.3 %collective-permute-start.101 = (bf16[4,256,512]{2,1,0:T(8,128)(2,1)}, bf16[4,256,512]{2,1,0:T(8,128)(2,1)}, u32[]{:S(2)}, u32[]{:S(2)}) collective-permute-start(bf16[4,256,512]{2,1,0:T(8,128)(2,1)} %get-tuple-element.494), channel_id=1, source_target_pairs={{0,4},{1,3},{2,6},{3,1},{4,0},{5,7},{6,2},{7,5},{8,12},{9,11},{10,... | collective-permute-start | bytes 3145736 | tf_op jit(solution)/shard_map/ppermute | solution.py:64
  799.4 65.0 %collective-permute-start.106 = (bf16[4,2048,512]{2,1,0:T(8,128)(2,1)}, bf16[4,2048,512]{2,1,0:T(8,128)(2,1)}, u32[]{:S(2)}, u32[]{:S(2)}) collective-permute-start(bf16[4,2048,512]{2,1,0:T(8,128)(2,1)} %get-tuple-element.506.g0_ref), channel_id=1, source_target_pairs={{0,1},{1,0},{2,3},{3,2},{4,5},{5,4},{6,7},{7,6},{8,9},{9,8},{10,11... | collective-permute-start | bytes 25165832 | tf_op jit(solution)/shard_map/ppermute | solution.py:64
  814.0 21.5 %collective-permute-start.104 = (bf16[4,256,512]{2,1,0:T(8,128)(2,1)}, bf16[4,256,512]{2,1,0:T(8,128)(2,1)}, u32[]{:S(2)}, u32[]{:S(2)}) collective-permute-start(bf16[4,256,512]{2,1,0:T(8,128)(2,1)} %get-tuple-element.500), channel_id=1, source_target_pairs={{0,4},{1,3},{2,6},{3,1},{4,0},{5,7},{6,2},{7,5},{8,12},{9,11},{10,... | collective-permute-start | bytes 3145736 | tf_op jit(solution)/shard_map/ppermute | solution.py:64
  835.6 47.5 %collective-permute-start.110 = (bf16[8,256,512]{2,1,0:T(8,128)(2,1)S(1)}, bf16[8,256,512]{2,1,0:T(8,128)(2,1)}, u32[]{:S(2)}, u32[]{:S(2)}) collective-permute-start(bf16[8,256,512]{2,1,0:T(8,128)(2,1)S(1)} %slice.641), channel_id=1, source_target_pairs={{0,2},{1,5},{2,0},{3,7},{4,6},{5,1},{6,4},{7,3},{8,10},{9,13},{10,... | collective-permute-start | bytes 6291464 | tf_op jit(solution)/shard_map/ppermute | solution.py:64
  839.6 24.9 %collective-permute-start.107 = (bf16[256,512]{1,0:T(8,128)(2,1)}, bf16[256,512]{1,0:T(8,128)(2,1)}, u32[]{:S(2)}, u32[]{:S(2)}) collective-permute-start(bf16[256,512]{1,0:T(8,128)(2,1)} %get-tuple-element.698), channel_id=1, source_target_pairs={{0,8},{1,9},{2,10},{3,11},{4,12},{5,13},{6,14},{7,15},{8,0},{9,1},... | collective-permute-start | bytes 786440 | tf_op jit(solution)/shard_map/ppermute | solution.py:64
  841.0 23.4 %collective-permute-start.108 = (bf16[256,512]{1,0:T(8,128)(2,1)}, bf16[256,512]{1,0:T(8,128)(2,1)}, u32[]{:S(2)}, u32[]{:S(2)}) collective-permute-start(bf16[256,512]{1,0:T(8,128)(2,1)} %get-tuple-element.697), channel_id=1, source_target_pairs={{0,16},{1,17},{2,18},{3,19},{4,20},{5,21},{6,22},{7,23},{8,24},{9,... | collective-permute-start | bytes 786440 | tf_op jit(solution)/shard_map/ppermute | solution.py:64
  843.4 21.1 %collective-permute-start.109 = (bf16[256,512]{1,0:T(8,128)(2,1)}, bf16[256,512]{1,0:T(8,128)(2,1)}, u32[]{:S(2)}, u32[]{:S(2)}) collective-permute-start(bf16[256,512]{1,0:T(8,128)(2,1)} %get-tuple-element.696), channel_id=1, source_target_pairs={{0,24},{1,25},{2,26},{3,27},{4,28},{5,29},{6,30},{7,31},{8,16},{9,... | collective-permute-start | bytes 786440 | tf_op jit(solution)/shard_map/ppermute | solution.py:64
  864.5 18.6 %collective-permute-start.111 = (bf16[4,9,16,256]{3,2,1,0:T(8,128)(2,1)}, bf16[4,9,16,256]{3,2,1,0:T(8,128)(2,1)S(1)}, u32[]{:S(2)}, u32[]{:S(2)}) collective-permute-start(bf16[4,9,16,256]{3,2,1,0:T(8,128)(2,1)} %get-tuple-element.512), channel_id=1, source_target_pairs={{0,4},{1,3},{2,6},{3,1},{4,0},{5,7},{6,2},{7,5},{8,12},{9,11},{10,... | collective-permute-start | bytes 884744 | tf_op jit(solution)/shard_map/ppermute | solution.py:64
  883.1 44.5 %collective-permute-start.112 = (bf16[8,256,512]{2,1,0:T(8,128)(2,1)}, bf16[8,256,512]{2,1,0:T(8,128)(2,1)}, u32[]{:S(2)}, u32[]{:S(2)}) collective-permute-start(bf16[8,256,512]{2,1,0:T(8,128)(2,1)} %shard_map.342), channel_id=1, source_target_pairs={{0,2},{1,5},{2,0},{3,7},{4,6},{5,1},{6,4},{7,3},{8,10},{9,13},{10,... | collective-permute-start | bytes 6291464 | tf_op jit(solution)/shard_map/ppermute | solution.py:64
  884.6 43.0 %collective-permute-start.113 = (bf16[256,512]{1,0:T(8,128)(2,1)}, bf16[256,512]{1,0:T(8,128)(2,1)}, u32[]{:S(2)}, u32[]{:S(2)}) collective-permute-start(bf16[256,512]{1,0:T(8,128)(2,1)} %get-tuple-element.519), channel_id=1, source_target_pairs={{0,8},{1,9},{2,10},{3,11},{4,12},{5,13},{6,14},{7,15},{8,0},{9,1},... | collective-permute-start | bytes 786440 | tf_op jit(solution)/shard_map/ppermute | solution.py:64
  887.0 40.6 %collective-permute-start.114 = (bf16[256,512]{1,0:T(8,128)(2,1)}, bf16[256,512]{1,0:T(8,128)(2,1)}, u32[]{:S(2)}, u32[]{:S(2)}) collective-permute-start(bf16[256,512]{1,0:T(8,128)(2,1)} %get-tuple-element.520), channel_id=1, source_target_pairs={{0,16},{1,17},{2,18},{3,19},{4,20},{5,21},{6,22},{7,23},{8,24},{9,... | collective-permute-start | bytes 786440 | tf_op jit(solution)/shard_map/ppermute | solution.py:64
  888.5 39.2 %collective-permute-start.115 = (bf16[256,512]{1,0:T(8,128)(2,1)}, bf16[256,512]{1,0:T(8,128)(2,1)}, u32[]{:S(2)}, u32[]{:S(2)}) collective-permute-start(bf16[256,512]{1,0:T(8,128)(2,1)} %get-tuple-element.521), channel_id=1, source_target_pairs={{0,24},{1,25},{2,26},{3,27},{4,28},{5,29},{6,30},{7,31},{8,16},{9,... | collective-permute-start | bytes 786440 | tf_op jit(solution)/shard_map/ppermute | solution.py:64
  893.6 34.1 %collective-permute-start.116 = (bf16[4,256,512]{2,1,0:T(8,128)(2,1)}, bf16[4,256,512]{2,1,0:T(8,128)(2,1)}, u32[]{:S(2)}, u32[]{:S(2)}) collective-permute-start(bf16[4,256,512]{2,1,0:T(8,128)(2,1)} %get-tuple-element.670), channel_id=1, source_target_pairs={{0,4},{1,3},{2,6},{3,1},{4,0},{5,7},{6,2},{7,5},{8,12},{9,11},{10,... | collective-permute-start | bytes 3145736 | tf_op jit(solution)/shard_map/ppermute | solution.py:64
  931.2 30.0 %collective-permute-start.117 = (bf16[4,256,512]{2,1,0:T(8,128)(2,1)}, bf16[4,256,512]{2,1,0:T(8,128)(2,1)S(1)}, u32[]{:S(2)}, u32[]{:S(2)}) collective-permute-start(bf16[4,256,512]{2,1,0:T(8,128)(2,1)} %get-tuple-element.678), channel_id=1, source_target_pairs={{0,4},{1,3},{2,6},{3,1},{4,0},{5,7},{6,2},{7,5},{8,12},{9,11},{10,... | collective-permute-start | bytes 3145736 | tf_op jit(solution)/shard_map/ppermute | solution.py:64
  938.4 18.3 %collective-permute-start.118 = (bf16[256,512]{1,0:T(8,128)(2,1)}, bf16[256,512]{1,0:T(8,128)(2,1)S(1)}, u32[]{:S(2)}, u32[]{:S(2)}) collective-permute-start(bf16[256,512]{1,0:T(8,128)(2,1)} %get-tuple-element.692), channel_id=1, source_target_pairs={{0,8},{1,9},{2,10},{3,11},{4,12},{5,13},{6,14},{7,15},{8,0},{9,1},... | collective-permute-start | bytes 786440 | tf_op jit(solution)/shard_map/ppermute | solution.py:64
  939.5 21.7 %collective-permute-start.119 = (bf16[256,512]{1,0:T(8,128)(2,1)}, bf16[256,512]{1,0:T(8,128)(2,1)}, u32[]{:S(2)}, u32[]{:S(2)}) collective-permute-start(bf16[256,512]{1,0:T(8,128)(2,1)} %get-tuple-element.691), channel_id=1, source_target_pairs={{0,16},{1,17},{2,18},{3,19},{4,20},{5,21},{6,22},{7,23},{8,24},{9,... | collective-permute-start | bytes 786440 | tf_op jit(solution)/shard_map/ppermute | solution.py:64
  941.8 19.4 %collective-permute-start.120 = (bf16[256,512]{1,0:T(8,128)(2,1)}, bf16[256,512]{1,0:T(8,128)(2,1)}, u32[]{:S(2)}, u32[]{:S(2)}) collective-permute-start(bf16[256,512]{1,0:T(8,128)(2,1)} %get-tuple-element.690), channel_id=1, source_target_pairs={{0,24},{1,25},{2,26},{3,27},{4,28},{5,29},{6,30},{7,31},{8,16},{9,... | collective-permute-start | bytes 786440 | tf_op jit(solution)/shard_map/ppermute | solution.py:64
  961.2 26.0 %collective-permute-start.121 = (bf16[9,16,256]{2,1,0:T(8,128)(2,1)}, bf16[9,16,256]{2,1,0:T(8,128)(2,1)S(1)}, u32[]{:S(2)}, u32[]{:S(2)}) collective-permute-start(bf16[9,16,256]{2,1,0:T(8,128)(2,1)} %get-tuple-element.541), channel_id=1, source_target_pairs={{0,8},{1,9},{2,10},{3,11},{4,12},{5,13},{6,14},{7,15},{8,0},{9,1},... | collective-permute-start | bytes 221192 | tf_op jit(solution)/shard_map/ppermute | solution.py:64
  991.4 23.1 %collective-permute-start.128 = (bf16[256,512]{1,0:T(8,128)(2,1)S(1)}, bf16[256,512]{1,0:T(8,128)(2,1)S(1)}, u32[]{:S(2)}, u32[]{:S(2)}) collective-permute-start(bf16[256,512]{1,0:T(8,128)(2,1)S(1)} %get-tuple-element.688), channel_id=1, source_target_pairs={{0,16},{1,17},{2,18},{3,19},{4,20},{5,21},{6,22},{7,23},{8,24},{9,... | collective-permute-start | bytes 786440 | tf_op jit(solution)/shard_map/ppermute | solution.py:64
  995.5 19.0 %collective-permute-start.129 = (bf16[256,512]{1,0:T(8,128)(2,1)S(1)}, bf16[256,512]{1,0:T(8,128)(2,1)S(1)}, u32[]{:S(2)}, u32[]{:S(2)}) collective-permute-start(bf16[256,512]{1,0:T(8,128)(2,1)S(1)} %get-tuple-element.687), channel_id=1, source_target_pairs={{0,24},{1,25},{2,26},{3,27},{4,28},{5,29},{6,30},{7,31},{8,16},{9,... | collective-permute-start | bytes 786440 | tf_op jit(solution)/shard_map/ppermute | solution.py:64
  999.9 44.6 %collective-permute-start.130 = (f32[2,9,14,252]{3,2,1,0:T(8,128)}, f32[2,9,14,252]{3,2,1,0:T(8,128)}, u32[]{:S(2)}, u32[]{:S(2)}) collective-permute-start(f32[2,9,14,252]{3,2,1,0:T(8,128)} %pad_maximum_fusion.8), channel_id=1, source_target_pairs={{0,3},{1,2},{2,1},{3,0},{4,7},{5,6},{6,5},{7,4},{8,11},{9,10},{10,... | collective-permute-start | bytes 762056 | tf_op jit(solution)/shard_map/ppermute | solution.py:64
  999.9 44.7 %collective-permute-start.131 = (f32[2,9,14,252]{3,2,1,0:T(8,128)}, f32[2,9,14,252]{3,2,1,0:T(8,128)}, u32[]{:S(2)}, u32[]{:S(2)}) collective-permute-start(f32[2,9,14,252]{3,2,1,0:T(8,128)} %pad_maximum_fusion.8), channel_id=1, source_target_pairs={{0,2},{1,3},{2,0},{3,1},{4,6},{5,7},{6,4},{7,5},{8,10},{9,11},{10,... | collective-permute-start | bytes 762056 | tf_op jit(solution)/shard_map/ppermute | solution.py:64
  1000.9 43.7 %collective-permute-start.132 = (f32[2,9,14,252]{3,2,1,0:T(8,128)}, f32[2,9,14,252]{3,2,1,0:T(8,128)}, u32[]{:S(2)}, u32[]{:S(2)}) collective-permute-start(f32[2,9,14,252]{3,2,1,0:T(8,128)} %pad_maximum_fusion.8), channel_id=1, source_target_pairs={{0,1},{1,0},{2,3},{3,2},{4,5},{5,4},{6,7},{7,6},{8,9},{9,8},{10,11... | collective-permute-start | bytes 762056 | tf_op jit(solution)/shard_map/ppermute | solution.py:64
  (182 other events, 1959.8 us)
Sparse Core Ops, SparseCore 0:
  13.3 108.4 all-gather.6
  138.6 102.5 all-gather.8
  255.3 80.9 all-gather.10
